TPU v7x, 128 devices: a whole 4x4x4 slice. The times are simulated.
128 devices in a mesh: role: 2 (over core), shard: 64 (over x, y, z).
Axes of the slice: x: 4, y: 4, z: 4, core: 2. Of those that a mesh axis runs over, the one named last changes fastest.
Arguments:
- query: bfloat16 [512, 8192], P('shard', 'role'), may hold values from -5 to 5, as said below
- fresh_token_keys: bfloat16 [512, 512], P('shard', 'role'), may hold values from -4 to 4
- fresh_token_values: bfloat16 [512, 512], P('shard', 'role'), may hold values from -4 to 4
- stored_keys: bfloat16 [512, 1024, 512], P('shard', None, 'role'), may hold values from -5 to 5, as said below
- stored_values: bfloat16 [512, 1024, 512], P('shard', None, 'role'), may hold values from -4 to 4
- slot_cache_length: int32 [512], P('shard'), may hold values from 2 to 1024, as said below
- residual: bfloat16 [512, 8192], P('shard', 'role'), may hold values from -6 to 6
- prenorm_scale: bfloat16 [8192], replicated, may hold values from 0.5 to 1.5
- request_cache_slot: int32 [512], replicated, may hold values from 0 to 511, each once
- request_adapter: int32 [512], replicated, may hold values from 0 to 255
- gate_projection_levels: bfloat16 [8192, 32768], P(None, ('role', 'shard')), may hold values from -8 to 7, as said below
- gate_group_scales: float32 [64, 32768], P(None, ('role', 'shard')), may hold values from 0.0012153398 to 0.0049718446
- up_projection_levels: bfloat16 [8192, 32768], P(None, ('role', 'shard')), may hold values from -8 to 7, as said below
- up_group_scales: float32 [64, 32768], P(None, ('role', 'shard')), may hold values from 0.0012153398 to 0.0049718446
- down_projection_levels: bfloat16 [32768, 8192], P(('role', 'shard')), may hold values from -8 to 7, as said below
- down_group_scales: float32 [256, 8192], P(('role', 'shard')), may hold values from 0.0006076699 to 0.002375437
- adapter_input_maps: bfloat16 [256, 16, 8192], P(('role', 'shard')), may hold values from -0.0625 to 0.0625
- adapter_gate_maps: bfloat16 [256, 16, 32768], P(None, None, ('role', 'shard')), may hold values from -1.5 to 1.5
Outputs:
- layer_out: bfloat16 [512, 8192], P(('role', 'shard'))
Inputs may be any that keep to these rules, and one draw needn't show every extreme that they name: `query`: entries are bounded in size. `stored_keys`: entries are bounded in size. `slot_cache_length`: some slot holds exactly 1024 cached tokens. `gate_projection_levels`: whole numbers. `up_projection_levels`: whole numbers. `down_projection_levels`: whole numbers.
All inputs are finite; a program needn't handle non-finite values.
Results may differ from a plain program's by a relative error of at most 0.01.
Values may be sent and summed in bfloat16 or wider, within the bound.
No kernel may reach another device: no remote copies, remote signals or barrier semaphores. Data moves between devices by JAX's collectives and lax.ppermute only.
A program may use at most 192 MiB of HBM per device.

v0:
```python
import jax
import jax.numpy as jnp
from jax import lax
from jax.sharding import PartitionSpec as P

HD = 128


def attend(
    query,
    fresh_token_keys,
    fresh_token_values,
    stored_keys,
    stored_values,
    slot_cache_length,
    kv_heads,
    head_dim,
):
    rows = query.shape[0]
    length = stored_keys.shape[1]
    groups = query.shape[1] // (kv_heads * head_dim)
    queries = query.reshape(rows, kv_heads, groups, head_dim)
    keys = stored_keys.reshape(rows, length, kv_heads, head_dim)
    values = stored_values.reshape(rows, length, kv_heads, head_dim)
    own_keys = fresh_token_keys.reshape(rows, kv_heads, head_dim)
    own_values = fresh_token_values.reshape(rows, kv_heads, head_dim)
    factor = head_dim ** (-0.5)
    scores = (
        jnp.einsum("skgd,slkd->skgl", queries, keys, preferred_element_type=jnp.float32) * factor
    )
    valid = jnp.arange(length)[None, :] < slot_cache_length[:, None]
    scores = jnp.where(valid[:, None, None, :], scores, -1e30)
    own = (
        jnp.einsum("skgd,skd->skg", queries, own_keys, preferred_element_type=jnp.float32) * factor
    )
    top = jnp.maximum(jnp.max(scores, axis=-1), own)
    weights = jnp.exp(scores - top[..., None])
    own_weight = jnp.exp(own - top)
    total = jnp.sum(weights, axis=-1) + own_weight
    mixed = jnp.einsum(
        "skgl,slkd->skgd", weights.astype(jnp.bfloat16), values, preferred_element_type=jnp.float32
    )
    mixed = (
        mixed
        + own_weight.astype(jnp.bfloat16).astype(jnp.float32)[..., None]
        * own_values.astype(jnp.float32)[:, :, None, :]
    )
    return (mixed / total[..., None]).reshape(rows, -1)


def dequant(levels, scales):
    count, cols = levels.shape
    blocks = scales.shape[0]
    wide = levels.reshape(blocks, count // blocks, cols).astype(jnp.float32) * scales[:, None, :]
    return wide.reshape(count, cols).astype(jnp.bfloat16)


def norm_rows(stream, prenorm_scale):
    wide = stream.astype(jnp.float32)
    meansq = jnp.mean(wide * wide, axis=-1, keepdims=True)
    return (wide * lax.rsqrt(meansq + 1e-05) * prenorm_scale.astype(jnp.float32)).astype(
        jnp.bfloat16
    )


def local(
    query,
    fresh_token_keys,
    fresh_token_values,
    stored_keys,
    stored_values,
    slot_cache_length,
    residual,
    prenorm_scale,
    request_cache_slot,
    request_adapter,
    gate_projection_levels,
    gate_group_scales,
    up_projection_levels,
    up_group_scales,
    down_projection_levels,
    down_group_scales,
    adapter_input_maps,
    adapter_gate_maps,
):
    local_heads = stored_keys.shape[2] // HD
    attended = attend(
        query,
        fresh_token_keys,
        fresh_token_values,
        stored_keys,
        stored_values,
        slot_cache_length,
        local_heads,
        HD,
    )
    stream = (residual.astype(jnp.float32) + attended).astype(jnp.bfloat16)
    joined = lax.all_gather(stream, "role", axis=1, tiled=True)
    whole = lax.all_gather(joined, "shard", axis=0, tiled=True)
    total_rows = whole.shape[0]
    normed = norm_rows(whole, prenorm_scale)
    sorted_entries = jnp.take(normed, request_cache_slot, axis=0)
    n_role = lax.axis_size("role")
    n_shard = lax.axis_size("shard")
    position = lax.axis_index("role") * n_shard + lax.axis_index("shard")
    resident_count = adapter_input_maps.shape[0]
    first = position * resident_count
    adapter_reduced = jnp.einsum(
        "vi,jli->vjl", sorted_entries, adapter_input_maps, preferred_element_type=jnp.float32
    )
    owned = request_adapter[:, None] == first + jnp.arange(resident_count, dtype=jnp.int32)[None, :]
    low_part = jnp.sum(jnp.where(owned[:, :, None], adapter_reduced, 0.0), axis=1)
    low = lax.psum(low_part, ("role", "shard")).astype(jnp.bfloat16)
    w_gate = dequant(gate_projection_levels, gate_group_scales)
    w_up = dequant(up_projection_levels, up_group_scales)
    w_down = dequant(down_projection_levels, down_group_scales)
    per_device = total_rows // (n_role * n_shard)
    row_table = jnp.arange(total_rows, dtype=jnp.int32)
    x_blk = jnp.take(sorted_entries, row_table, axis=0)
    low_blk = jnp.take(low, row_table, axis=0)
    identifiers = jnp.take(request_adapter, row_table, axis=0)
    selected_entries = jnp.take(adapter_gate_maps, identifiers, axis=0)
    delta = jnp.einsum("nr,nrf->nf", low_blk, selected_entries, preferred_element_type=jnp.float32)
    gate = jnp.dot(x_blk, w_gate, preferred_element_type=jnp.float32) + 2.0 * delta
    up = jnp.dot(x_blk, w_up, preferred_element_type=jnp.float32)
    hidden = (jax.nn.silu(gate) * up).astype(jnp.bfloat16)
    mine = lax.psum_scatter(
        jnp.dot(hidden, w_down, preferred_element_type=jnp.float32),
        ("role", "shard"),
        scatter_dimension=0,
        tiled=True,
    )
    my_rows = position * per_device + jnp.arange(per_device, dtype=jnp.int32)
    my_slots = jnp.take(request_cache_slot, my_rows, axis=0)
    own_stream = jnp.take(whole, my_slots, axis=0)
    return (own_stream.astype(jnp.float32) + mine).astype(jnp.bfloat16)


def solution(mesh):
    return jax.shard_map(
        local,
        mesh=mesh,
        in_specs=(
            P("shard", "role"),
            P("shard", "role"),
            P("shard", "role"),
            P("shard", None, "role"),
            P("shard", None, "role"),
            P("shard"),
            P("shard", "role"),
            P(),
            P(),
            P(),
            P(None, ("role", "shard")),
            P(None, ("role", "shard")),
            P(None, ("role", "shard")),
            P(None, ("role", "shard")),
            P(("role", "shard"), None),
            P(("role", "shard"), None),
            P(("role", "shard"), None, None),
            P(None, None, ("role", "shard")),
        ),
        out_specs=P(("role", "shard"), None),
        check_vma=False,
    )
```

profile of v0, /device:TPU:1, one launch (start us, length us, event | category | flops | bytes accessed | tf_op | source)
XLA Modules:
  0.0 492.7 jit_solution(18382101842318302726)
XLA Ops:
  8.2 1.0 fusion.55
  9.1 3.5 fusion.67
  13.0 3.0 fusion.39
  16.1 3.1 all_gather.6
  19.4 3.5 gather_fusion.3
  23.0 3.5 gather_fusion.4
  26.4 5.2 %fusion.7 = bf16[8192,256]{1,0:T(8,128)(2,1)} fusion(bf16[8192,256]{1,0:T(8,128)(2,1)} %param.30, f32[64,256]{1,0:T(8,128)S(1)} %copy-done.6), kind=kLoop, calls=%fused_computation.19 | loop fusion | flops 6291456 | bytes 8454144 | tf_op jit(solution)/shard_map/convert_element_type | solution.py:55
  31.7 2.9 fusion.4
  34.6 2.8 fusion.3
  37.6 62.7 %all-gather.2.cloned.1.call-done = bf16[512,8192]{1,0:T(8,128)(2,1)} async-done(((bf16[8,8192]{1,0:T(8,128)(2,1)}), bf16[512,8192]{1,0:T(8,128)(2,1)}) %all-gather.2.cloned.1.call-update) | async-done | bytes 8388624 | tf_op jit(solution)/shard_map/all_gather | solution.py:99
  100.3 5.1 %fusion = f32[512]{0:T(512)S(1)} fusion(bf16[512,8192]{1,0:T(8,128)(2,1)} %all-gather.2.cloned.1.call-done), kind=kLoop, calls=%fused_computation.9 | loop fusion | flops 12582400 | bytes 8390656 | tf_op jit(solution)/shard_map/reduce_sum | solution.py:60
  105.4 9.9 %fusion.2 = bf16[512,8192]{1,0:T(8,128)(2,1)} fusion(bf16[512,8192]{1,0:T(8,128)(2,1)} %all-gather.2.cloned.1.call-done, f32[8192]{0:T(1024)S(1)} %convert_element_type.76, f32[512]{0:T(512)S(1)} %add_rsqrt_fusion), kind=kLoop, calls=%fused_computation.11 | loop fusion | flops 16777216 | bytes 16812032 | tf_op jit(solution)/shard_map/convert_element_type | solution.py:61
  115.3 20.4 %gather_fusion.5 = bf16[512,8192]{1,0:T(8,128)(2,1)} fusion(bf16[512,8192]{1,0:T(8,128)(2,1)} %fusion.2, s32[1024]{0:T(1024)S(1)} %pad_clamp_fusion.2), kind=kCustom, calls=%fused_computation.clone | custom fusion | bytes 16779264 | tf_op jit(solution)/shard_map/jit(_take)/gather | solution.py:102
  135.6 7.5 %broadcast_select_fusion.1 = bf16[512,8192]{1,0:T(8,128)(2,1)} fusion(bf16[512,8192]{1,0:T(8,128)(2,1)} %gather_fusion.5, pred[512]{0:T(512)(128)(4,1)S(1)} %compare_and_fusion), kind=kLoop, calls=%fused_computation.21 | loop fusion | flops 4194304 | bytes 16777728 | tf_op jit(solution)/shard_map/jit(_take)/select_n | solution.py:102
  143.1 20.2 %gather_fusion.6 = bf16[512,8192]{1,0:T(8,128)(2,1)} fusion(bf16[512,8192]{1,0:T(8,128)(2,1)} %broadcast_select_fusion.1, s32[1024]{0:T(1024)S(1)} %pad_clamp_fusion.1), kind=kCustom, calls=%fused_computation.1.clone | custom fusion | bytes 16779264 | tf_op jit(solution)/shard_map/jit(_take)/gather | solution.py:119
  163.3 6.0 %fusion.36 = f32[512,16]{0,1:T(8,128)S(1)} fusion(bf16[2,16,8192]{2,1,0:T(8,128)(2,1)S(1)} %copy-done.11, bf16[512,8192]{1,0:T(8,128)(2,1)} %broadcast_select_fusion.1, pred[512,2]{0,1:T(4,128)(4,1)S(1)} %broadcast_compare_fusion), kind=kOutput, calls=%fused_computation.42 | convolution fusion | flops 268460032 | bytes 8946688 | tf_op jit(solution)/shard_map/vi,jli->vjl/dot_general | solution.py:108
  169.4 65.8 %psum.7 = bf16[512,16]{1,0:T(8,128)(2,1)S(1)} all-reduce(f32[512,16]{1,0:T(8,128)S(1)} %copy.35), channel_id=1, replica_groups=mesh['role'=2,'shard'=64] {'role','shard'}, use_global_device_ids=true, to_apply=%region_4.6 | all-reduce | flops 8192 | bytes 49152 | tf_op jit(solution)/shard_map/psum | solution.py:113
  235.2 1.3 gather_fusion.2
  236.7 5.7 %fusion.14 = f32[512,1,256]{2,1,0:T(1,128)S(1)} fusion(bf16[512,16,256]{2,1,0:T(8,128)(2,1)} %gather_fusion.4, pred[512]{0:T(512)(128)(4,1)S(1)} %compare_and_fusion.1, bf16[512,16,1]{1,0,2:T(8,128)(2,1)S(1)} %select_bitcast_fusion), kind=kOutput, calls=%fused_computation.28 | convolution fusion | flops 6291456 | bytes 4735488 | tf_op jit(solution)/shard_map/nr,nrf->nf/dot_general | solution.py:123
  242.4 7.0 %fusion.26 = f32[512,256]{1,0:T(8,128)S(1)} fusion(bf16[8192,256]{1,0:T(8,128)(2,1)} %fusion.7, bf16[512,8192]{1,0:T(8,128)(2,1)} %gather_fusion.6, pred[512]{0:T(512)(128)(4,1)S(1)} %broadcast_compare_fusion.1, f32[512,1,256]{2,1,0:T(1,128)S(1)} %fusion.14), kind=kOutput, calls=%fused_computation.36 | convolution fusion | flops 2151940096 | bytes 13632000 | tf_op jit(solution)/shard_map/dot_general | solution.py:124
  249.4 20.4 %fusion.29 = f32[512,8192]{1,0:T(8,128)} fusion(bf16[256,8192]{1,0:T(8,128)(2,1)} %fusion.3, bf16[8192,256]{1,0:T(8,128)(2,1)} %fusion.4, bf16[512,8192]{1,0:T(8,128)(2,1)} %gather_fusion.6, pred[512]{0:T(512)(128)(4,1)S(1)} %broadcast_compare_fusion.1, f32[512,256]{1,0:T(8,128)S(1)} %fusion.26), kind=kOutput, calls=%fused_computation.39 | convolution fusion | flops 4299948032 | bytes 34079232 | tf_op jit(solution)/shard_map/dot_general | solution.py:128
  270.6 5.1 %gather_fusion.1 = bf16[4,8192]{1,0:T(4,128)(2,1)S(1)} fusion(bf16[512,8192]{1,0:T(8,128)(2,1)} %all-gather.2.cloned.1.call-done, s32[1024]{0:T(1024)S(1)} %pad_clamp_fusion.3), kind=kCustom, calls=%fused_computation.3 | custom fusion | bytes 131088 | tf_op jit(solution)/shard_map/jit(_take)/gather | solution.py:135
  275.7 208.2 %all-reduce.3.cloned.1.call-done = f32[512,8192]{1,0:T(8,128)} async-done(((f32[512,8192]{1,0:T(8,128)}), f32[512,8192]{1,0:T(8,128)}) %all-reduce.3.cloned.1.call-update) | async-done | bytes 16777232
  483.9 1.7 fusion.54
  (56 shorter events, 3.2 us)
Async XLA Ops:
  6.5 16.4 %copy-start = (bf16[256,16,256]{2,1,0:T(8,128)(2,1)S(1)}, bf16[256,16,256]{2,1,0:T(8,128)(2,1)}, u32[]{:S(2)}) copy-start(bf16[256,16,256]{2,1,0:T(8,128)(2,1)} %param.37) | copy-start | bytes 6291460
  6.5 9.5 %copy-start.9 = (bf16[8,4096]{1,0:T(8,128)(2,1)S(1)}, bf16[8,4096]{1,0:T(8,128)(2,1)}, u32[]{:S(2)}) copy-start(bf16[8,4096]{1,0:T(8,128)(2,1)} %param.26) | copy-start | bytes 196612
  6.5 12.8 %copy-start.10 = (bf16[8192]{0:T(1024)(128)(2,1)S(1)}, bf16[8192]{0:T(1024)(128)(2,1)}, u32[]{:S(2)}) copy-start(bf16[8192]{0:T(1024)(128)(2,1)} %param.27) | copy-start | bytes 49156
  6.5 12.8 %copy-start.2 = (s32[512]{0:T(512)S(1)}, s32[512]{0:T(512)}, u32[]{:S(2)}) copy-start(s32[512]{0:T(512)} %param.29) | copy-start | bytes 6148
  6.5 93.8 %all-gather.2.cloned.1.call-start = ((), (), s32[]{:S(2)}) async-start(), calls=%async_computation | async-start | bytes 8519680 | tf_op jit(solution)/shard_map/all_gather | solution.py:99
  13.0 13.4 %copy-start.6 = (f32[64,256]{1,0:T(8,128)S(1)}, f32[64,256]{1,0:T(8,128)}, u32[]{:S(2)}) copy-start(f32[64,256]{1,0:T(8,128)} %param.31) | copy-start | bytes 196612
  19.3 464.6 %all-reduce.3.cloned.1.call-start = ((), (), s32[]{:S(2)}) async-start(), calls=%async_computation.1 | async-start | bytes 33554432
  22.9 8.7 %copy-start.7 = (f32[64,256]{1,0:T(8,128)S(1)}, f32[64,256]{1,0:T(8,128)}, u32[]{:S(2)}) copy-start(f32[64,256]{1,0:T(8,128)} %param.33) | copy-start | bytes 196612
  26.4 5.3 %copy-start.4 = (bf16[8192,256]{1,0:T(8,128)(2,1)S(1)}, bf16[8192,256]{1,0:T(8,128)(2,1)}, u32[]{:S(2)}) copy-start(bf16[8192,256]{1,0:T(8,128)(2,1)} %param.32) | copy-start | bytes 12582916
  26.4 8.2 %copy-start.5 = (bf16[256,8192]{1,0:T(8,128)(2,1)S(1)}, bf16[256,8192]{1,0:T(8,128)(2,1)}, u32[]{:S(2)}) copy-start(bf16[256,8192]{1,0:T(8,128)(2,1)} %param.34) | copy-start | bytes 12582916
  26.4 8.2 %copy-start.8 = (f32[2,8192]{1,0:T(2,128)S(1)}, f32[2,8192]{1,0:T(2,128)}, u32[]{:S(2)}) copy-start(f32[2,8192]{1,0:T(2,128)} %param.35) | copy-start | bytes 196612
  31.7 5.8 %copy-start.3 = (s32[512]{0:T(512)S(1)}, s32[512]{0:T(512)}, u32[]{:S(2)}) copy-start(s32[512]{0:T(512)} %param.28) | copy-start | bytes 6148
  143.1 20.2 %copy-start.11 = (bf16[2,16,8192]{2,1,0:T(8,128)(2,1)S(1)}, bf16[2,16,8192]{2,1,0:T(8,128)(2,1)}, u32[]{:S(2)}) copy-start(bf16[2,16,8192]{2,1,0:T(8,128)(2,1)} %param.36) | copy-start | bytes 1572868
  269.8 215.8 %copy-start.1 = (bf16[256,16,256]{2,1,0:T(8,128)(2,1)S(1)}, bf16[256,16,256]{2,1,0:T(8,128)(2,1)}, u32[]{:S(2)}) copy-start(bf16[256,16,256]{2,1,0:T(8,128)(2,1)} %param.37) | copy-start | bytes 6291460
Sparse Core Ops, SparseCore 0:
  19.4 80.8 all-gather.1
  270.0 213.9 all-reduce.2
where the time goes:
time: 502 us; the launch traced here: 493 us
  waiting for transfers between devices  271 us (54%)
  blocking collectives  68.9 us (14%)
  local copies, waits for them, and re-layouts  54.8 us (11%)
  matrix products  46.6 us (9%)
  other arithmetic  37.4 us (7%)
  between operations  13.9 us (3%)
    unnamed x3, waiting for transfers between devices  208 us
    psum x1, blocking collectives, local(): low = lax.psum(low_part, ('role', 'shard')).astype(jnp.bfloat16)  65.8 us
    all_gather x1, waiting for transfers between devices, local(): whole = lax.all_gather(joined, 'shard', axis=0, tiled=True)  62.7 us
    dot_general x1, matrix products, local(): jnp.dot(hidden, w_down, preferred_element_type=jnp.float32)  20.4 us
    gather x1, local copies, waits for them, and re-layouts, local(): sorted_entries = jnp.take(normed, request_cache_slot, axis=0)  20.4 us
    gather x1, local copies, waits for them, and re-layouts, local(): x_blk = jnp.take(sorted_entries, row_table, axis=0)  20.2 us
    convert_element_type x3, other arithmetic, dequant(): return wide.reshape(count, cols).astype(jnp.bfloat16)  11 us
  transfers between devices with their start and end apart: 2, of which 2 were waited for; matrix products, arithmetic and copies ran while one was open for 5% of the time, Pallas kernels for 0%

commit v1 on v0

v1 whole, which is shorter than its diff:
```python
import functools

import jax
import jax.numpy as jnp
from jax import lax
from jax.experimental import pallas as pl
from jax.experimental.pallas import tpu as pltpu
from jax.sharding import PartitionSpec as P

HD = 128
BF = jnp.bfloat16
F32 = jnp.float32
AXES = ((2, 1, 0), (2, 0, 1))


def attend(
    query,
    fresh_token_keys,
    fresh_token_values,
    stored_keys,
    stored_values,
    slot_cache_length,
    kv_heads,
    head_dim,
):
    rows = query.shape[0]
    length = stored_keys.shape[1]
    groups = query.shape[1] // (kv_heads * head_dim)
    queries = query.reshape(rows, kv_heads, groups, head_dim)
    keys = stored_keys.reshape(rows, length, kv_heads, head_dim)
    values = stored_values.reshape(rows, length, kv_heads, head_dim)
    own_keys = fresh_token_keys.reshape(rows, kv_heads, head_dim)
    own_values = fresh_token_values.reshape(rows, kv_heads, head_dim)
    factor = head_dim ** (-0.5)
    scores = jnp.einsum("skgd,slkd->skgl", queries, keys, preferred_element_type=F32) * factor
    valid = jnp.arange(length)[None, :] < slot_cache_length[:, None]
    scores = jnp.where(valid[:, None, None, :], scores, -1e30)
    own = jnp.einsum("skgd,skd->skg", queries, own_keys, preferred_element_type=F32) * factor
    top = jnp.maximum(jnp.max(scores, axis=-1), own)
    weights = jnp.exp(scores - top[..., None])
    own_weight = jnp.exp(own - top)
    total = jnp.sum(weights, axis=-1) + own_weight
    mixed = jnp.einsum("skgl,slkd->skgd", weights.astype(BF), values, preferred_element_type=F32)
    mixed = (
        mixed
        + own_weight.astype(BF).astype(F32)[..., None] * own_values.astype(F32)[:, :, None, :]
    )
    return (mixed / total[..., None]).reshape(rows, -1)


def dequant(levels, scales):
    count, cols = levels.shape
    blocks = scales.shape[0]
    wide = levels.reshape(blocks, count // blocks, cols).astype(F32) * scales[:, None, :]
    return wide.reshape(count, cols).astype(BF)


def chip_index(coords):
    return coords[0] * 16 + coords[1] * 4 + coords[2]


def shift_perm(phase, step):
    pairs = []
    for role in range(2):
        axis = AXES[role][phase]
        for x in range(4):
            for y in range(4):
                for z in range(4):
                    here = [x, y, z]
                    there = list(here)
                    there[axis] = (there[axis] + step) % 4
                    pairs.append((role * 64 + chip_index(here), role * 64 + chip_index(there)))
    return pairs


def send(value, phase, step):
    return lax.ppermute(value, ("role", "shard"), shift_perm(phase, step))


def swap(value):
    return lax.ppermute(value, "role", [(0, 1), (1, 0)])


def ring(value, phase):
    return [value] + [send(value, phase, step) for step in (1, 2, 3)]


def ring_forward(value, phase):
    half = value.shape[0] // 2
    a, b = value[:half], value[half:]
    up_a = send(a, phase, 1)
    down_b = send(b, phase, -1)
    up_b = send(b, phase, 1)
    down_a = send(a, phase, -1)
    far_a = send(up_a, phase, 1)
    far_b = send(down_b, phase, -1)
    cat = lambda p, q: jnp.concatenate([p, q], axis=0)
    return [value, cat(up_a, up_b), cat(far_a, far_b), cat(down_a, down_b)]


def pick(table, index):
    hit = index[:, None] == jnp.arange(table.shape[0], dtype=jnp.int32)[None, :]
    return jnp.sum(jnp.where(hit, table[None, :], 0), axis=1)


def hidden_kernel(o0, o1, o2, o3, r0, r1, r2, r3, low_ref, inv_ref, ids_ref, maps_ref, out_ref):
    own, other = (o0, o1, o2, o3), (r0, r1, r2, r3)
    low = low_ref[...]
    ids = ids_ref[...]
    group = lax.broadcasted_iota(jnp.int32, low.shape, 1) // 16
    rest = ids - group
    acc = jnp.zeros(out_ref.shape, F32)
    for j in range(16):
        parts = [jnp.where(rest == 8 * (2 * j + i), low, 0.0).astype(BF) for i in range(2)]
        lhs = jnp.concatenate(parts, axis=1)
        acc = acc + jnp.dot(lhs, maps_ref[j * 256 : (j + 1) * 256, :], preferred_element_type=F32)
    width = out_ref.shape[1]
    for d3 in range(4):
        for d2 in range(4):
            mine = own[d3][d2 * 32 : (d2 + 1) * 32, :] + other[d2][d3 * 32 : (d3 + 1) * 32, :]
            row = (d3 * 4 + d2) * 32
            inv = inv_ref[row : row + 32, :]
            inv = jnp.concatenate([inv] * (width // 128), axis=1)
            gate = mine[:, :width] * inv + 2.0 * acc[row : row + 32, :]
            up = mine[:, width:] * inv
            out_ref[row : row + 32, :] = (gate / (1.0 + jnp.exp(-gate)) * up).astype(BF)


def make_hidden(own, other, low, inv, ids, maps):
    rows = 512
    width = maps.shape[1]
    return pl.pallas_call(
        hidden_kernel,
        out_shape=jax.ShapeDtypeStruct((rows, width), BF),
        compiler_params=pltpu.CompilerParams(vmem_limit_bytes=40 * 1024 * 1024),
        cost_estimate=pl.CostEstimate(
            flops=2 * rows * 4096 * width, bytes_accessed=7 * 1024 * 1024, transcendentals=rows * width
        ),
    )(*own, *other, low, inv, ids, maps)


def local(
    query,
    fresh_token_keys,
    fresh_token_values,
    stored_keys,
    stored_values,
    slot_cache_length,
    residual,
    prenorm_scale,
    request_cache_slot,
    request_adapter,
    gate_projection_levels,
    gate_group_scales,
    up_projection_levels,
    up_group_scales,
    down_projection_levels,
    down_group_scales,
    adapter_input_maps,
    adapter_gate_maps,
):
    role = lax.axis_index("role")
    shard = lax.axis_index("shard")
    here = (shard // 16, (shard // 4) % 4, shard % 4)
    half = residual.shape[1]
    units = gate_projection_levels.shape[1]
    first = role == 0

    def axis_of(mine, phase):
        a, b = AXES[0][phase], AXES[1][phase]
        return (a, b) if mine else (b, a)

    def by_role(pair, values):
        return jnp.where(first, values[pair[0]], values[pair[1]])

    def position(slot, mine):
        q = slot // 8
        chip = (q // 16, (q // 4) % 4, q % 4)
        total = 0
        for phase in (2, 1, 0):
            pair = axis_of(mine, phase)
            total = total * 4 + (by_role(pair, here) - by_role(pair, chip)) % 4
        return total * 8 + slot % 8

    every = jnp.arange(512, dtype=jnp.int32)
    pos_of_request = position(request_cache_slot, True)
    hit_row = pos_of_request[None, :] == every[:, None]
    adapter_of_row = jnp.sum(jnp.where(hit_row, request_adapter[None, :], 0), axis=1)
    steps = [every // 128, (every // 32) % 4, (every // 8) % 4]
    coords = [None] * 3
    for axis in range(3):
        value = 0
        for place, phase in enumerate((2, 1, 0)):
            pair = axis_of(True, phase)
            mine = jnp.where(first, pair[0], pair[1]) == axis
            value = value + jnp.where(mine, steps[place], 0)
        coords[axis] = (here[axis] + value) % 4
    lane = every % 8
    request = (lane // 4) * 256 + chip_index(coords) * 4 + lane % 4
    slot = pick(request_cache_slot, request)
    pick_mine = (position(slot, True)[:, None] == every[None, :]).astype(BF)
    pick_other = (position(slot, False)[:, None] == every[None, :]).astype(BF)

    gain = prenorm_scale.astype(F32)
    maps = (adapter_input_maps.astype(F32) * gain).astype(BF).reshape(-1, 2 * half)
    maps_keep = lax.dynamic_slice(maps, (0, role * half), (maps.shape[0], half))
    maps_send = lax.dynamic_slice(maps, (0, (1 - role) * half), (maps.shape[0], half))
    maps_chip = jnp.concatenate([maps_keep, swap(maps_send)], axis=0)
    maps_line = jnp.concatenate(ring(maps_chip, 2), axis=0)
    entry = jnp.arange(16, dtype=jnp.int32)
    far = entry // 4
    last = axis_of(True, 2)
    line_coords = [
        jnp.where(jnp.where(first, last[0], last[1]) == axis, (here[axis] - far) % 4, here[axis])
        for axis in range(3)
    ]
    line_role = jnp.where((entry // 2) % 2 == 0, role, 1 - role)
    line_ids = (line_role * 64 + chip_index(line_coords)) * 2 + entry % 2

    attended = attend(
        query,
        fresh_token_keys,
        fresh_token_values,
        stored_keys,
        stored_values,
        slot_cache_length,
        stored_keys.shape[2] // HD,
        HD,
    )
    stream = (residual.astype(F32) + attended).astype(BF)

    line = jnp.concatenate(ring(stream, 0), axis=0)
    plane = jnp.concatenate(ring(line, 1), axis=0)

    def half_weights(levels, scales, which):
        rows = levels.shape[0] // 2
        lev = lax.dynamic_slice(levels, (which * rows, 0), (rows, levels.shape[1]))
        sc = lax.dynamic_slice(scales, (which * (scales.shape[0] // 2), 0), (scales.shape[0] // 2, levels.shape[1]))
        g = lax.dynamic_slice(gain, (which * rows,), (rows,))
        return (dequant(lev, sc).astype(F32) * g[:, None]).astype(BF)

    def both(which):
        return jnp.concatenate(
            [
                half_weights(gate_projection_levels, gate_group_scales, which),
                half_weights(up_projection_levels, up_group_scales, which),
            ],
            axis=1,
        )

    w_send = both(1 - role)
    w_keep = both(role)
    w_recv = swap(w_send)

    def half_down(which):
        lev = lax.dynamic_slice(down_projection_levels, (0, which * half), (units, half))
        sc = lax.dynamic_slice(down_group_scales, (0, which * half), (down_group_scales.shape[0], half))
        return dequant(lev, sc)

    down_recv = swap(half_down(1 - role))
    w_down = jnp.concatenate([half_down(role), down_recv], axis=0)

    blocks = ring_forward(plane, 2)
    own, other = [], []
    for block in blocks:
        other.append(swap(jnp.dot(block, w_recv, preferred_element_type=F32)))
        own.append(jnp.dot(block, w_keep, preferred_element_type=F32))

    products = lax.dot_general(maps_line, plane, (((1,), (1,)), ((), ())), preferred_element_type=F32)
    products = products.reshape(16, 16, 128)
    owned = line_ids[:, None] == adapter_of_row[None, :128]
    low = jnp.sum(jnp.where(owned[:, None, :], products, 0.0), axis=0)
    for phase, size in ((0, 8), (1, 32)):
        parts = ring(low, phase)
        low = parts[0]
        for step in (1, 2, 3):
            wide = parts[step].reshape(16, 128 // (4 * size), 4, size)
            low = low + jnp.roll(wide, step, axis=2).reshape(16, 128)
    wide = plane.astype(F32)
    square = jnp.sum(wide * wide, axis=1)
    extended = jnp.concatenate([low, jnp.broadcast_to(square[None, :], (8, 128))], axis=0)
    extended = jnp.concatenate(ring(extended, 2), axis=1)
    partner = swap(extended).reshape(24, 4, 4, 32).transpose(0, 2, 1, 3).reshape(24, 512)
    extended = extended + partner
    inv = lax.rsqrt(extended[16] / (2 * half) + 1e-05)
    low = (extended[:16] * inv[None, :]).astype(BF).astype(F32)
    low8 = jnp.tile(low.T, (1, 8))
    inv_wide = jnp.broadcast_to(inv[:, None], (512, 128))
    ids_wide = jnp.broadcast_to(adapter_of_row[:, None], (512, 128))

    hidden = make_hidden(own, other, low8, inv_wide, ids_wide, adapter_gate_maps.reshape(-1, units))
    hidden_other = swap(hidden)

    mine = jnp.dot(pick_mine, hidden, preferred_element_type=F32).astype(BF)
    theirs = jnp.dot(pick_other, hidden_other, preferred_element_type=F32).astype(BF)
    both_hidden = jnp.concatenate([mine, theirs], axis=1)

    def product(step):
        return jnp.dot(both_hidden[step * 128 : (step + 1) * 128], w_down, preferred_element_type=F32)

    b2 = product(2).astype(BF)
    far_a = send(b2[:64], 2, 1)
    far_b = send(b2[64:], 2, -1)
    b1 = product(1)
    b3 = product(3)
    near_b = send(b1[64:].astype(BF), 2, 1)
    near_a = send(b3[:64].astype(BF), 2, -1)
    b0 = product(0)
    via_a = send((b1[:64] + far_a.astype(F32)).astype(BF), 2, 1)
    via_b = send((b3[64:] + far_b.astype(F32)).astype(BF), 2, -1)
    sum_a = b0[:64] + via_a.astype(F32) + near_a.astype(F32)
    sum_b = b0[64:] + via_b.astype(F32) + near_b.astype(F32)
    part = [sum_a[:32], sum_a[32:], sum_b[:32], sum_b[32:]]
    for phase, size in ((1, 32), (0, 8)):
        got = [send(part[step].astype(BF), phase, step) for step in (2, 1, 3)]
        total = part[0] + got[0].astype(F32) + got[1].astype(F32) + got[2].astype(F32)
        part = [total[i * (size // 4) : (i + 1) * (size // 4)] for i in range(4)]
    rows8 = pick_mine[:8]
    base = sum(
        jnp.dot(rows8[:, d * 128 : (d + 1) * 128], blocks[d], preferred_element_type=F32) for d in range(4)
    )
    result = (base + total).astype(BF)
    keep = lax.dynamic_slice(result, (role * 4, 0), (4, half))
    got = swap(lax.dynamic_slice(result, ((1 - role) * 4, 0), (4, half)))
    return jnp.concatenate([jnp.where(first, keep, got), jnp.where(first, got, keep)], axis=1)


def solution(mesh):
    return jax.shard_map(
        local,
        mesh=mesh,
        in_specs=(
            P("shard", "role"),
            P("shard", "role"),
            P("shard", "role"),
            P("shard", None, "role"),
            P("shard", None, "role"),
            P("shard"),
            P("shard", "role"),
            P(),
            P(),
            P(),
            P(None, ("role", "shard")),
            P(None, ("role", "shard")),
            P(None, ("role", "shard")),
            P(None, ("role", "shard")),
            P(("role", "shard"), None),
            P(("role", "shard"), None),
            P(("role", "shard"), None, None),
            P(None, None, ("role", "shard")),
        ),
        out_specs=P(("role", "shard"), None),
        check_vma=False,
    )
```

time: 502 us -> 191 us (0.38); the launches traced: 493 us -> 190 us
  waiting for transfers between devices: 271 us -> 53.9 us
  blocking collectives: 68.9 us -> 0 us
  starting transfers between devices: 0.08 us -> 64.2 us
  local copies, waits for them, and re-layouts: 54.8 us -> 14.7 us
  other arithmetic: 37.4 us -> 19.7 us
  between operations: 13.9 us -> 1.01 us
  matrix products: 46.6 us -> 35.6 us
    unnamed x3 -> x0, waiting for transfers between devices: 208 us -> none
    psum x1 -> x0, blocking collectives: 65.8 us -> none  [local(): low = lax.psum(low_part, ('role', 'shard')).astype(jnp.bfloat16)]
    ppermute x0 -> x46, starting transfers between devices: none -> 64.2 us  [the longest x36 45.1 us: send(): return lax.ppermute(value, ('role', 'shard'), shift_perm(phase, step))]
    all_gather x1 -> x0, waiting for transfers between devices: 62.7 us -> none  [local(): whole = lax.all_gather(joined, 'shard', axis=0, tiled=True)]
    gather x7 -> x0, local copies, waits for them, and re-layouts: 54.6 us -> none  [the longest x1 20.4 us: local(): sorted_entries = jnp.take(normed, request_cache_slot, axis=0)]
    ppermute x0 -> x46, waiting for transfers between devices: none -> 53.9 us  [the longest x36 51.5 us: send(): return lax.ppermute(value, ('role', 'shard'), shift_perm(phase, step))]
    convert_element_type x9 -> x8, other arithmetic: 23.5 us -> 10.1 us  [the longest x1 5.77 us: half_weights(): return (dequant(lev, sc).astype(F32) * g[:, None]).astype(BF)]
    dot_general x7 -> x22, matrix products: 46.6 us -> 35.6 us  [the longest x4 12.6 us: local(): other.append(swap(jnp.dot(block, w_recv, preferred_element_type=F32)))]
  transfers between devices with their start and end apart: 2 -> 46, of which waited for: 2 -> 16; matrix products, arithmetic and copies ran while one was open for 5% -> 30% of each run, Pallas kernels for 0% -> 1%
where the time goes in v1:
time: 191 us; the launch traced here: 190 us
  starting transfers between devices  64.2 us (34%)
  waiting for transfers between devices  53.9 us (28%)
  matrix products  35.6 us (19%)
  other arithmetic  19.7 us (10%)
  local copies, waits for them, and re-layouts  14.7 us (8%)
    ppermute x36, waiting for transfers between devices, send(): return lax.ppermute(value, ('role', 'shard'), shift_perm(phase, step))  51.5 us
    ppermute x36, starting transfers between devices, send(): return lax.ppermute(value, ('role', 'shard'), shift_perm(phase, step))  45.1 us
    ppermute x10, starting transfers between devices, swap(): return lax.ppermute(value, 'role', [(0, 1), (1, 0)])  19.1 us
    dot_general x4, matrix products, local(): other.append(swap(jnp.dot(block, w_recv, preferred_element_type=F32)))  12.6 us
    dot_general x4, matrix products, product(): jnp.dot(both_hidden[step * 128:(step + 1) * 128], w_down, preferred_eleme...  9.34 us
    unnamed x73, local copies, waits for them, and re-layouts  8.76 us
    convert_element_type x1, other arithmetic, half_weights(): return (dequant(lev, sc).astype(F32) * g[:, None]).astype(BF)  5.77 us
    dot_general x4, matrix products, local(): own.append(jnp.dot(block, w_keep, preferred_element_type=F32))  5.3 us
  transfers between devices with their start and end apart: 46, of which 16 were waited for; matrix products, arithmetic and copies ran while one was open for 30% of the time, Pallas kernels for 1%

profile of v1, /device:TPU:1, one launch (start us, length us, event | category | flops | bytes accessed | tf_op | source)
XLA Modules:
  0.0 190.4 jit_solution(11401746059017500099)
XLA Ops:
  2.3 3.5 %fusion.147 = (f32[8,2,16]{2,1,0:T(2,128)S(1)}, f32[8,2,16,1024]{3,2,1,0:T(8,128)S(1)}) fusion(bf16[8,2,16,128]{3,0,2,1:T(8,128)(2,1)} %bitcast.132, pred[8,1024]{1,0:T(8,128)(4,1)S(1)} %iota_compare_fusion.5, bf16[8,1024,256]{2,1,0:T(8,128)(2,1)} %param.21), kind=kOutput, calls=%fused_computation.350 | convolution fusion | flops 67895040 | bytes 5317632 | tf_op jit(solution)/shard_map/skgd,slkd->skgl/dot_general | solution.py:35
  9.6 3.3 %collective-permute-start.1 = (bf16[8,4096]{1,0:T(8,128)(2,1)S(1)}, bf16[8,4096]{1,0:T(8,128)(2,1)}, u32[]{:S(2)}, u32[]{:S(2)}) collective-permute-start(bf16[8,4096]{1,0:T(8,128)(2,1)S(1)} %get-tuple-element.13), channel_id=1, source_target_pairs={{0,2},{1,3},{2,0},{3,1},{4,6},{5,7},{6,4},{7,5},{8,10},{9,11},{10,... | collective-permute-start | bytes 196616 | tf_op jit(solution)/shard_map/ppermute | solution.py:77
  13.7 5.8 %multiply_convert_fusion = (bf16[4096,256]{1,0:T(8,128)(2,1)S(1)}, bf16[4096,256]{1,0:T(8,128)(2,1)}, bf16[4096,256]{1,0:T(8,128)(2,1)}, bf16[4096,256]{1,0:T(8,128)(2,1)S(1)}) fusion(f32[32,256]{1,0:T(8,128)S(1)} %get-tuple-element.44, bf16[8192,256]{1,0:T(8,128)(2,1)} %param.30, s32[]{:T(128)S(6)} %select_n.617, f32[4096]{0:T(1024)S(1)} %get-tuple-element.56, ...), kind=kLoop, calls=%fused_computation.27 | loop fusion | flops 25165824 | bytes 16941064 | tf_op jit(solution)/shard_map/convert_element_type | solution.py:240
  38.1 2.7 %collective-permute-start.19 = (bf16[64,4096]{1,0:T(8,128)(2,1)S(1)}, bf16[64,4096]{1,0:T(8,128)(2,1)S(1)}, u32[]{:S(2)}, u32[]{:S(2)}) collective-permute-start(bf16[64,4096]{1,0:T(8,128)(2,1)S(1)} %pad_maximum_fusion.3), channel_id=1, source_target_pairs={{0,32},{1,33},{2,34},{3,35},{4,36},{5,37},{6,38},{7,39},{8,40},{9,... | collective-permute-start | bytes 1572872 | tf_op jit(solution)/shard_map/ppermute | solution.py:77
  42.8 3.7 %collective-permute-done.18 = bf16[64,4096]{1,0:T(8,128)(2,1)S(1)} collective-permute-done((bf16[64,4096]{1,0:T(8,128)(2,1)S(1)}, bf16[64,4096]{1,0:T(8,128)(2,1)S(1)}, u32[]{:S(2)}, u32[]{:S(2)}) %collective-permute-start.18) | collective-permute-done | bytes 524320 | tf_op jit(solution)/shard_map/ppermute | solution.py:77
  46.4 6.8 %collective-permute-done.19 = bf16[64,4096]{1,0:T(8,128)(2,1)S(1)} collective-permute-done((bf16[64,4096]{1,0:T(8,128)(2,1)S(1)}, bf16[64,4096]{1,0:T(8,128)(2,1)S(1)}, u32[]{:S(2)}, u32[]{:S(2)}) %collective-permute-start.19) | collective-permute-done | bytes 524320 | tf_op jit(solution)/shard_map/ppermute | solution.py:77
  59.2 3.9 %collective-permute-done.21 = f32[16,128]{1,0:T(8,128)S(1)} collective-permute-done((f32[16,128]{1,0:T(8,128)S(1)}, f32[16,128]{1,0:T(8,128)S(1)}, u32[]{:S(2)}, u32[]{:S(2)}) %collective-permute-start.21) | collective-permute-done | bytes 8224 | tf_op jit(solution)/shard_map/ppermute | solution.py:77
  68.1 3.2 %collective-permute-done.24 = f32[16,128]{1,0:T(8,128)S(1)} collective-permute-done((f32[16,128]{1,0:T(8,128)S(1)}, f32[16,128]{1,0:T(8,128)S(1)}, u32[]{:S(2)}, u32[]{:S(2)}) %collective-permute-start.24) | collective-permute-done | bytes 8224 | tf_op jit(solution)/shard_map/ppermute | solution.py:77
  74.0 3.1 %fusion.137.o0 = f32[128,512]{1,0:T(8,128)S(1)} fusion(bf16[128,4096]{1,0:T(8,128)(2,1)S(1)} %get-tuple-element.30, bf16[4096,256]{1,0:T(8,128)(2,1)} %get-tuple-element.19, bf16[4096,256]{1,0:T(8,128)(2,1)} %get-tuple-element.52), kind=kOutput, calls=%fused_computation.342 | convolution fusion | flops 545259520 | bytes 5505024 | tf_op jit(solution)/shard_map/dot_general | solution.py:267
  77.1 7.2 %collective-permute-start.32 = (bf16[256,4096]{1,0:T(8,128)(2,1)}, bf16[256,4096]{1,0:T(8,128)(2,1)}, u32[]{:S(2)}, u32[]{:S(2)}) collective-permute-start(bf16[256,4096]{1,0:T(8,128)(2,1)} %get-tuple-element.15), channel_id=1, source_target_pairs={{0,64},{64,0},{1,65},{65,1},{2,66},{66,2},{3,67},{67,3},{4,68},{68... | collective-permute-start | bytes 6291464 | tf_op jit(solution)/shard_map/ppermute | solution.py:81
  88.6 5.7 %collective-permute-done.7 = bf16[64,4096]{1,0:T(8,128)(2,1)S(1)} collective-permute-done((bf16[64,4096]{1,0:T(8,128)(2,1)S(1)}, bf16[64,4096]{1,0:T(8,128)(2,1)S(1)}, u32[]{:S(2)}, u32[]{:S(2)}) %collective-permute-start.7) | collective-permute-done | bytes 524320 | tf_op jit(solution)/shard_map/ppermute | solution.py:77
  94.3 3.3 %collective-permute-start.30 = (f32[24,512]{1,0:T(8,128)S(1)}, f32[24,512]{1,0:T(8,128)S(1)}, u32[]{:S(2)}, u32[]{:S(2)}) collective-permute-start(f32[24,512]{1,0:T(8,128)S(1)} %pad_maximum_fusion.11), channel_id=1, source_target_pairs={{0,64},{64,0},{1,65},{65,1},{2,66},{66,2},{3,67},{67,3},{4,68},{68... | collective-permute-start | bytes 147464 | tf_op jit(solution)/shard_map/ppermute | solution.py:81
  104.0 6.6 %collective-permute-done.8 = bf16[64,4096]{1,0:T(8,128)(2,1)} collective-permute-done((bf16[64,4096]{1,0:T(8,128)(2,1)}, bf16[64,4096]{1,0:T(8,128)(2,1)}, u32[]{:S(2)}, u32[]{:S(2)}) %collective-permute-start.8) | collective-permute-done | bytes 524320 | tf_op jit(solution)/shard_map/ppermute | solution.py:77
  112.8 3.6 %fusion.148 = f32[128,512]{1,0:T(8,128)S(1)} fusion(bf16[128,4096]{1,0:T(8,128)(2,1)} %copy-done.3, bf16[4096,512]{1,0:T(8,128)(2,1)} %collective-permute-done.12), kind=kOutput, calls=%fused_computation.351 | convolution fusion | flops 536870912 | bytes 5505024 | tf_op jit(solution)/shard_map/dot_general | solution.py:266
  118.7 3.0 %fusion.149 = f32[128,512]{1,0:T(8,128)S(1)} fusion(bf16[128,4096]{1,0:T(8,128)(2,1)S(1)} %copy-done.6, bf16[4096,512]{1,0:T(8,128)(2,1)} %collective-permute-done.12), kind=kOutput, calls=%fused_computation.352 | convolution fusion | flops 536870912 | bytes 5505024 | tf_op jit(solution)/shard_map/dot_general | solution.py:266
  121.8 3.1 %fusion.150 = f32[128,512]{1,0:T(8,128)S(1)} fusion(bf16[128,4096]{1,0:T(8,128)(2,1)S(1)} %constant_dynamic-update-slice_fusion.16, bf16[4096,512]{1,0:T(8,128)(2,1)} %collective-permute-done.12), kind=kOutput, calls=%fused_computation.353 | convolution fusion | flops 536870912 | bytes 5505024 | tf_op jit(solution)/shard_map/dot_general | solution.py:266
  125.5 3.0 %fusion.151 = f32[128,512]{1,0:T(8,128)S(1)} fusion(bf16[128,4096]{1,0:T(8,128)(2,1)S(1)} %copy-done.11, bf16[4096,512]{1,0:T(8,128)(2,1)} %collective-permute-done.12), kind=kOutput, calls=%fused_computation.354 | convolution fusion | flops 536870912 | bytes 5505024 | tf_op jit(solution)/shard_map/dot_general | solution.py:266
  139.0 2.7 %collective-permute-start.35 = (bf16[64,4096]{1,0:T(8,128)(2,1)S(1)}, bf16[64,4096]{1,0:T(8,128)(2,1)}, u32[]{:S(2)}, u32[]{:S(2)}) collective-permute-start(bf16[64,4096]{1,0:T(8,128)(2,1)S(1)} %slice.297), channel_id=1, source_target_pairs={{0,48},{1,49},{2,50},{3,51},{4,52},{5,53},{6,54},{7,55},{8,56},{9,... | collective-permute-start | bytes 1572872 | tf_op jit(solution)/shard_map/ppermute | solution.py:77
  144.9 2.7 %collective-permute-start.36 = (bf16[64,4096]{1,0:T(8,128)(2,1)S(1)}, bf16[64,4096]{1,0:T(8,128)(2,1)S(1)}, u32[]{:S(2)}, u32[]{:S(2)}) collective-permute-start(bf16[64,4096]{1,0:T(8,128)(2,1)S(1)} %get-tuple-element.23), channel_id=1, source_target_pairs={{0,48},{1,49},{2,50},{3,51},{4,52},{5,53},{6,54},{7,55},{8,56},{9,... | collective-permute-start | bytes 1572872 | tf_op jit(solution)/shard_map/ppermute | solution.py:77
  148.5 5.2 %collective-permute-done.36 = bf16[64,4096]{1,0:T(8,128)(2,1)S(1)} collective-permute-done((bf16[64,4096]{1,0:T(8,128)(2,1)S(1)}, bf16[64,4096]{1,0:T(8,128)(2,1)S(1)}, u32[]{:S(2)}, u32[]{:S(2)}) %collective-permute-start.36) | collective-permute-done | bytes 524320 | tf_op jit(solution)/shard_map/ppermute | solution.py:77
  154.7 3.5 %collective-permute-start.37 = (bf16[64,4096]{1,0:T(8,128)(2,1)}, bf16[64,4096]{1,0:T(8,128)(2,1)}, u32[]{:S(2)}, u32[]{:S(2)}) collective-permute-start(bf16[64,4096]{1,0:T(8,128)(2,1)} %fusion.27), channel_id=1, source_target_pairs={{0,48},{1,49},{2,50},{3,51},{4,52},{5,53},{6,54},{7,55},{8,56},{9,... | collective-permute-start | bytes 1572872 | tf_op jit(solution)/shard_map/ppermute | solution.py:77
  160.8 3.8 %collective-permute-done.37 = bf16[64,4096]{1,0:T(8,128)(2,1)} collective-permute-done((bf16[64,4096]{1,0:T(8,128)(2,1)}, bf16[64,4096]{1,0:T(8,128)(2,1)}, u32[]{:S(2)}, u32[]{:S(2)}) %collective-permute-start.37) | collective-permute-done | bytes 524320 | tf_op jit(solution)/shard_map/ppermute | solution.py:77
  171.9 6.2 %collective-permute-done.40 = bf16[32,4096]{1,0:T(8,128)(2,1)S(1)} collective-permute-done((bf16[32,4096]{1,0:T(8,128)(2,1)S(1)}, bf16[32,4096]{1,0:T(8,128)(2,1)S(1)}, u32[]{:S(2)}, u32[]{:S(2)}) %collective-permute-start.40) | collective-permute-done | bytes 262176 | tf_op jit(solution)/shard_map/ppermute | solution.py:77
  185.3 3.5 %collective-permute-start.45 = (bf16[4,4096]{1,0:T(4,128)(2,1)S(1)}, bf16[4,4096]{1,0:T(4,128)(2,1)S(1)}, u32[]{:S(2)}, u32[]{:S(2)}) collective-permute-start(bf16[4,4096]{1,0:T(4,128)(2,1)S(1)} %constant_dynamic-slice_fusion.8), channel_id=1, source_target_pairs={{0,64},{64,0},{1,65},{65,1},{2,66},{66,2},{3,67},{67,3},{4,68},{68... | collective-permute-start | bytes 98312 | tf_op jit(solution)/shard_map/ppermute | solution.py:81
  (252 shorter events, 90.6 us)
Async XLA Ops:
  7.1 19.3 %collective-permute-start = (bf16[8,4096]{1,0:T(8,128)(2,1)S(1)}, bf16[8,4096]{1,0:T(8,128)(2,1)}, u32[]{:S(2)}, u32[]{:S(2)}) collective-permute-start(bf16[8,4096]{1,0:T(8,128)(2,1)S(1)} %get-tuple-element.13), channel_id=1, source_target_pairs={{0,1},{1,2},{2,3},{3,0},{4,5},{5,6},{6,7},{7,4},{8,9},{9,10},{10,1... | collective-permute-start | bytes 196616 | tf_op jit(solution)/shard_map/ppermute | solution.py:77
  9.6 16.7 %collective-permute-start.1 = (bf16[8,4096]{1,0:T(8,128)(2,1)S(1)}, bf16[8,4096]{1,0:T(8,128)(2,1)}, u32[]{:S(2)}, u32[]{:S(2)}) collective-permute-start(bf16[8,4096]{1,0:T(8,128)(2,1)S(1)} %get-tuple-element.13), channel_id=1, source_target_pairs={{0,2},{1,3},{2,0},{3,1},{4,6},{5,7},{6,4},{7,5},{8,10},{9,11},{10,... | collective-permute-start | bytes 196616 | tf_op jit(solution)/shard_map/ppermute | solution.py:77
  13.0 13.5 %collective-permute-start.2 = (bf16[8,4096]{1,0:T(8,128)(2,1)S(1)}, bf16[8,4096]{1,0:T(8,128)(2,1)S(1)}, u32[]{:S(2)}, u32[]{:S(2)}) collective-permute-start(bf16[8,4096]{1,0:T(8,128)(2,1)S(1)} %get-tuple-element.13), channel_id=1, source_target_pairs={{0,3},{1,0},{2,1},{3,2},{4,7},{5,4},{6,5},{7,6},{8,11},{9,8},{10,9... | collective-permute-start | bytes 196616 | tf_op jit(solution)/shard_map/ppermute | solution.py:77
  21.9 90.9 %collective-permute-start.12 = (bf16[4096,512]{1,0:T(8,128)(2,1)}, bf16[4096,512]{1,0:T(8,128)(2,1)}, u32[]{:S(2)}, u32[]{:S(2)}) collective-permute-start(bf16[4096,512]{1,0:T(8,128)(2,1)} %pad_maximum_fusion.1), channel_id=1, source_target_pairs={{0,64},{64,0},{1,65},{65,1},{2,66},{66,2},{3,67},{67,3},{4,68},{68... | collective-permute-start | bytes 12582920 | tf_op jit(solution)/shard_map/ppermute | solution.py:81
  24.4 11.4 %collective-permute-start.17 = (bf16[32,4096]{1,0:T(8,128)(2,1)}, bf16[32,4096]{1,0:T(8,128)(2,1)S(1)}, u32[]{:S(2)}, u32[]{:S(2)}) collective-permute-start(bf16[32,4096]{1,0:T(8,128)(2,1)} %get-tuple-element.26), channel_id=1, source_target_pairs={{0,64},{64,0},{1,65},{65,1},{2,66},{66,2},{3,67},{67,3},{4,68},{68... | collective-permute-start | bytes 786440 | tf_op jit(solution)/shard_map/ppermute | solution.py:81
  27.3 10.8 %collective-permute-start.3 = (bf16[32,4096]{1,0:T(8,128)(2,1)S(1)}, bf16[32,4096]{1,0:T(8,128)(2,1)S(1)}, u32[]{:S(2)}, u32[]{:S(2)}) collective-permute-start(bf16[32,4096]{1,0:T(8,128)(2,1)S(1)} %pad_maximum_fusion.4), channel_id=1, source_target_pairs={{0,4},{1,5},{2,6},{3,7},{4,8},{5,9},{6,10},{7,11},{8,12},{9,13},{1... | collective-permute-start | bytes 786440 | tf_op jit(solution)/shard_map/ppermute | solution.py:77
  28.6 13.0 %collective-permute-start.4 = (bf16[32,4096]{1,0:T(8,128)(2,1)S(1)}, bf16[32,4096]{1,0:T(8,128)(2,1)S(1)}, u32[]{:S(2)}, u32[]{:S(2)}) collective-permute-start(bf16[32,4096]{1,0:T(8,128)(2,1)S(1)} %pad_maximum_fusion.4), channel_id=1, source_target_pairs={{0,8},{1,9},{2,10},{3,11},{4,12},{5,13},{6,14},{7,15},{8,0},{9,1},... | collective-permute-start | bytes 786440 | tf_op jit(solution)/shard_map/ppermute | solution.py:77
  31.0 11.6 %collective-permute-start.5 = (bf16[32,4096]{1,0:T(8,128)(2,1)S(1)}, bf16[32,4096]{1,0:T(8,128)(2,1)S(1)}, u32[]{:S(2)}, u32[]{:S(2)}) collective-permute-start(bf16[32,4096]{1,0:T(8,128)(2,1)S(1)} %pad_maximum_fusion.4), channel_id=1, source_target_pairs={{0,12},{1,13},{2,14},{3,15},{4,0},{5,1},{6,2},{7,3},{8,4},{9,5},{1... | collective-permute-start | bytes 786440 | tf_op jit(solution)/shard_map/ppermute | solution.py:77
  38.1 15.1 %collective-permute-start.19 = (bf16[64,4096]{1,0:T(8,128)(2,1)S(1)}, bf16[64,4096]{1,0:T(8,128)(2,1)S(1)}, u32[]{:S(2)}, u32[]{:S(2)}) collective-permute-start(bf16[64,4096]{1,0:T(8,128)(2,1)S(1)} %pad_maximum_fusion.3), channel_id=1, source_target_pairs={{0,32},{1,33},{2,34},{3,35},{4,36},{5,37},{6,38},{7,39},{8,40},{9,... | collective-permute-start | bytes 1572872 | tf_op jit(solution)/shard_map/ppermute | solution.py:77
  41.6 11.7 %collective-permute-start.20 = (bf16[64,4096]{1,0:T(8,128)(2,1)S(1)}, bf16[64,4096]{1,0:T(8,128)(2,1)S(1)}, u32[]{:S(2)}, u32[]{:S(2)}) collective-permute-start(bf16[64,4096]{1,0:T(8,128)(2,1)S(1)} %pad_maximum_fusion.3), channel_id=1, source_target_pairs={{0,48},{1,49},{2,50},{3,51},{4,52},{5,53},{6,54},{7,55},{8,56},{9,... | collective-permute-start | bytes 1572872 | tf_op jit(solution)/shard_map/ppermute | solution.py:77
  65.4 20.3 %collective-permute-start.6 = (bf16[64,4096]{1,0:T(8,128)(2,1)}, bf16[64,4096]{1,0:T(8,128)(2,1)}, u32[]{:S(2)}, u32[]{:S(2)}) collective-permute-start(bf16[64,4096]{1,0:T(8,128)(2,1)} %get-tuple-element.35), channel_id=1, source_target_pairs={{0,16},{1,17},{2,18},{3,19},{4,20},{5,21},{6,22},{7,23},{8,24},{9,... | collective-permute-start | bytes 1572872 | tf_op jit(solution)/shard_map/ppermute | solution.py:77
  72.3 11.9 %collective-permute-start.28 = (f32[24,128]{1,0:T(8,128)S(1)}, f32[24,128]{1,0:T(8,128)S(1)}, u32[]{:S(2)}, u32[]{:S(2)}) collective-permute-start(f32[24,128]{1,0:T(8,128)S(1)} %pad_maximum_fusion.15), channel_id=1, source_target_pairs={{0,32},{1,33},{2,34},{3,35},{4,36},{5,37},{6,38},{7,39},{8,40},{9,... | collective-permute-start | bytes 36872 | tf_op jit(solution)/shard_map/ppermute | solution.py:77
  73.9 10.8 %collective-permute-start.27 = (f32[24,128]{1,0:T(8,128)S(1)}, f32[24,128]{1,0:T(8,128)S(1)}, u32[]{:S(2)}, u32[]{:S(2)}) collective-permute-start(f32[24,128]{1,0:T(8,128)S(1)} %pad_maximum_fusion.15), channel_id=1, source_target_pairs={{0,16},{1,17},{2,18},{3,19},{4,20},{5,21},{6,22},{7,23},{8,24},{9,... | collective-permute-start | bytes 36872 | tf_op jit(solution)/shard_map/ppermute | solution.py:77
  77.1 57.0 %collective-permute-start.32 = (bf16[256,4096]{1,0:T(8,128)(2,1)}, bf16[256,4096]{1,0:T(8,128)(2,1)}, u32[]{:S(2)}, u32[]{:S(2)}) collective-permute-start(bf16[256,4096]{1,0:T(8,128)(2,1)} %get-tuple-element.15), channel_id=1, source_target_pairs={{0,64},{64,0},{1,65},{65,1},{2,66},{66,2},{3,67},{67,3},{4,68},{68... | collective-permute-start | bytes 6291464 | tf_op jit(solution)/shard_map/ppermute | solution.py:81
  84.3 14.3 %collective-permute-start.11 = (bf16[64,4096]{1,0:T(8,128)(2,1)S(1)}, bf16[64,4096]{1,0:T(8,128)(2,1)S(1)}, u32[]{:S(2)}, u32[]{:S(2)}) collective-permute-start(bf16[64,4096]{1,0:T(8,128)(2,1)S(1)} %copy-done.25), channel_id=1, source_target_pairs={{0,48},{1,49},{2,50},{3,51},{4,52},{5,53},{6,54},{7,55},{8,56},{9,... | collective-permute-start | bytes 1572872 | tf_op jit(solution)/shard_map/ppermute | solution.py:77
  85.7 12.9 %collective-permute-start.9 = (bf16[64,4096]{1,0:T(8,128)(2,1)S(1)}, bf16[64,4096]{1,0:T(8,128)(2,1)}, u32[]{:S(2)}, u32[]{:S(2)}) collective-permute-start(bf16[64,4096]{1,0:T(8,128)(2,1)S(1)} %copy-done.21), channel_id=1, source_target_pairs={{0,48},{1,49},{2,50},{3,51},{4,52},{5,53},{6,54},{7,55},{8,56},{9,... | collective-permute-start | bytes 1572872 | tf_op jit(solution)/shard_map/ppermute | solution.py:77
  100.7 9.9 %collective-permute-start.8 = (bf16[64,4096]{1,0:T(8,128)(2,1)}, bf16[64,4096]{1,0:T(8,128)(2,1)}, u32[]{:S(2)}, u32[]{:S(2)}) collective-permute-start(bf16[64,4096]{1,0:T(8,128)(2,1)} %collective-permute-done.6), channel_id=1, source_target_pairs={{0,16},{1,17},{2,18},{3,19},{4,20},{5,21},{6,22},{7,23},{8,24},{9,... | collective-permute-start | bytes 1572872 | tf_op jit(solution)/shard_map/ppermute | solution.py:77
  100.7 10.9 %collective-permute-start.10 = (bf16[64,4096]{1,0:T(8,128)(2,1)}, bf16[64,4096]{1,0:T(8,128)(2,1)}, u32[]{:S(2)}, u32[]{:S(2)}) collective-permute-start(bf16[64,4096]{1,0:T(8,128)(2,1)} %collective-permute-done.9), channel_id=1, source_target_pairs={{0,48},{1,49},{2,50},{3,51},{4,52},{5,53},{6,54},{7,55},{8,56},{9,... | collective-permute-start | bytes 1572872 | tf_op jit(solution)/shard_map/ppermute | solution.py:77
  116.4 13.3 %collective-permute-start.13 = (f32[128,512]{1,0:T(8,128)S(1)}, f32[128,512]{1,0:T(8,128)S(1)}, u32[]{:S(2)}, u32[]{:S(2)}) collective-permute-start(f32[128,512]{1,0:T(8,128)S(1)} %fusion.148), channel_id=1, source_target_pairs={{0,64},{64,0},{1,65},{65,1},{2,66},{66,2},{3,67},{67,3},{4,68},{68... | collective-permute-start | bytes 786440 | tf_op jit(solution)/shard_map/ppermute | solution.py:81
  136.5 11.1 %collective-permute-start.33 = (bf16[64,4096]{1,0:T(8,128)(2,1)S(1)}, bf16[64,4096]{1,0:T(8,128)(2,1)S(1)}, u32[]{:S(2)}, u32[]{:S(2)}) collective-permute-start(bf16[64,4096]{1,0:T(8,128)(2,1)S(1)} %get-tuple-element.22), channel_id=1, source_target_pairs={{0,16},{1,17},{2,18},{3,19},{4,20},{5,21},{6,22},{7,23},{8,24},{9,... | collective-permute-start | bytes 1572872 | tf_op jit(solution)/shard_map/ppermute | solution.py:77
  139.0 21.8 %collective-permute-start.35 = (bf16[64,4096]{1,0:T(8,128)(2,1)S(1)}, bf16[64,4096]{1,0:T(8,128)(2,1)}, u32[]{:S(2)}, u32[]{:S(2)}) collective-permute-start(bf16[64,4096]{1,0:T(8,128)(2,1)S(1)} %slice.297), channel_id=1, source_target_pairs={{0,48},{1,49},{2,50},{3,51},{4,52},{5,53},{6,54},{7,55},{8,56},{9,... | collective-permute-start | bytes 1572872 | tf_op jit(solution)/shard_map/ppermute | solution.py:77
  144.9 15.8 %collective-permute-start.38 = (bf16[64,4096]{1,0:T(8,128)(2,1)}, bf16[64,4096]{1,0:T(8,128)(2,1)}, u32[]{:S(2)}, u32[]{:S(2)}) collective-permute-start(bf16[64,4096]{1,0:T(8,128)(2,1)} %slice.296), channel_id=1, source_target_pairs={{0,16},{1,17},{2,18},{3,19},{4,20},{5,21},{6,22},{7,23},{8,24},{9,... | collective-permute-start | bytes 1572872 | tf_op jit(solution)/shard_map/ppermute | solution.py:77
  148.5 12.2 %collective-permute-start.34 = (bf16[64,4096]{1,0:T(8,128)(2,1)}, bf16[64,4096]{1,0:T(8,128)(2,1)}, u32[]{:S(2)}, u32[]{:S(2)}) collective-permute-start(bf16[64,4096]{1,0:T(8,128)(2,1)} %fusion.30), channel_id=1, source_target_pairs={{0,16},{1,17},{2,18},{3,19},{4,20},{5,21},{6,22},{7,23},{8,24},{9,... | collective-permute-start | bytes 1572872 | tf_op jit(solution)/shard_map/ppermute | solution.py:77
  154.7 10.0 %collective-permute-start.37 = (bf16[64,4096]{1,0:T(8,128)(2,1)}, bf16[64,4096]{1,0:T(8,128)(2,1)}, u32[]{:S(2)}, u32[]{:S(2)}) collective-permute-start(bf16[64,4096]{1,0:T(8,128)(2,1)} %fusion.27), channel_id=1, source_target_pairs={{0,48},{1,49},{2,50},{3,51},{4,52},{5,53},{6,54},{7,55},{8,56},{9,... | collective-permute-start | bytes 1572872 | tf_op jit(solution)/shard_map/ppermute | solution.py:77
  (52 other events, 434.6 us)

commit v2 on v0

v2 whole, which is shorter than its diff:
```python
import functools

import jax
import jax.numpy as jnp
from jax import lax
from jax.experimental import pallas as pl
from jax.experimental.pallas import tpu as pltpu
from jax.sharding import PartitionSpec as P

HD = 128
BF = jnp.bfloat16
F32 = jnp.float32
AXES = ((2, 1, 0), (2, 0, 1))


def attend(
    query,
    fresh_token_keys,
    fresh_token_values,
    stored_keys,
    stored_values,
    slot_cache_length,
    kv_heads,
    head_dim,
):
    rows = query.shape[0]
    length = stored_keys.shape[1]
    groups = query.shape[1] // (kv_heads * head_dim)
    queries = query.reshape(rows, kv_heads, groups, head_dim)
    keys = stored_keys.reshape(rows, length, kv_heads, head_dim)
    values = stored_values.reshape(rows, length, kv_heads, head_dim)
    own_keys = fresh_token_keys.reshape(rows, kv_heads, head_dim)
    own_values = fresh_token_values.reshape(rows, kv_heads, head_dim)
    factor = head_dim ** (-0.5)
    scores = jnp.einsum("skgd,slkd->skgl", queries, keys, preferred_element_type=F32) * factor
    valid = jnp.arange(length)[None, :] < slot_cache_length[:, None]
    scores = jnp.where(valid[:, None, None, :], scores, -1e30)
    own = jnp.einsum("skgd,skd->skg", queries, own_keys, preferred_element_type=F32) * factor
    top = jnp.maximum(jnp.max(scores, axis=-1), own)
    weights = jnp.exp(scores - top[..., None])
    own_weight = jnp.exp(own - top)
    total = jnp.sum(weights, axis=-1) + own_weight
    mixed = jnp.einsum("skgl,slkd->skgd", weights.astype(BF), values, preferred_element_type=F32)
    mixed = (
        mixed
        + own_weight.astype(BF).astype(F32)[..., None] * own_values.astype(F32)[:, :, None, :]
    )
    return (mixed / total[..., None]).reshape(rows, -1)


def dequant(levels, scales):
    count, cols = levels.shape
    blocks = scales.shape[0]
    wide = levels.reshape(blocks, count // blocks, cols).astype(F32) * scales[:, None, :]
    return wide.reshape(count, cols).astype(BF)


def weights_kernel(role, gate_ref, gate_scale, up_ref, up_scale, gain_ref, down_ref, down_scale, ready, out_ref, keep_ref, send_ref, token):
    width = gate_ref.shape[1]
    for group in range(gate_ref.shape[0] // 128):
        rows = slice(group * 128, (group + 1) * 128)
        gain = jnp.broadcast_to(gain_ref[0:1, rows], (128, 128)).T
        gain = jnp.concatenate([gain] * (width // 128), axis=1)
        for place, (levels, scales) in enumerate(((gate_ref, gate_scale), (up_ref, up_scale))):
            wide = (levels[rows, :].astype(F32) * scales[group : group + 1, :]).astype(BF)
            out_ref[rows, place * width : (place + 1) * width] = (wide.astype(F32) * gain).astype(BF)
    i = pl.program_id(0)
    half = pl.num_programs(0) // 2
    for ref, here in ((keep_ref, i < half), (send_ref, i >= half)):

        @pl.when(here)
        def _():
            for group in range(down_ref.shape[0] // 128):
                rows = slice(group * 128, (group + 1) * 128)
                ref[rows, :] = (down_ref[rows, :].astype(F32) * down_scale[group : group + 1, :]).astype(BF)

    token[...] = jnp.zeros_like(token)


def make_weights(role, gate, gate_scales, up, up_scales, gain, down, down_scales, ready):
    depth, width = gate.shape
    step = 1024
    count = depth // step
    half = count // 2
    turned = lambda i, r: (i + r[0] * half) % count
    levels = pl.BlockSpec((step, width), lambda i, r: (turned(i, r), 0))
    scales = pl.BlockSpec((step // 128, width), lambda i, r: (turned(i, r), 0))
    across = lambda rows: pl.BlockSpec((rows, step), lambda i, r: (0, turned(i, r)))
    return pl.pallas_call(
        weights_kernel,
        out_shape=[
            jax.ShapeDtypeStruct((depth, 2 * width), BF),
            jax.ShapeDtypeStruct((width, depth // 2), BF),
            jax.ShapeDtypeStruct((width, depth // 2), BF),
            jax.ShapeDtypeStruct((16, 128), BF),
        ],
        grid_spec=pltpu.PrefetchScalarGridSpec(
            num_scalar_prefetch=1,
            grid=(count,),
            in_specs=[levels, scales, levels, scales, across(1), across(width), across(down_scales.shape[0]), pl.BlockSpec((8, 128), lambda i, r: (0, 0))],
            out_specs=[
                pl.BlockSpec((step, 2 * width), lambda i, r: (i, 0)),
                pl.BlockSpec((width, step), lambda i, r: (0, jnp.minimum(i, half - 1))),
                pl.BlockSpec((width, step), lambda i, r: (0, jnp.maximum(i - half, 0))),
                pl.BlockSpec((16, 128), lambda i, r: (0, 0)),
            ],
        ),
        compiler_params=pltpu.CompilerParams(vmem_limit_bytes=48 * 1024 * 1024),
        cost_estimate=pl.CostEstimate(flops=12 * depth * width, bytes_accessed=12 * depth * width, transcendentals=0),
    )(role.reshape(1), gate, gate_scales, up, up_scales, gain, down, down_scales, ready)


def chip_index(coords):
    return coords[0] * 16 + coords[1] * 4 + coords[2]


def shift_perm(phase, step):
    pairs = []
    for role in range(2):
        axis = AXES[role][phase]
        for x in range(4):
            for y in range(4):
                for z in range(4):
                    here = [x, y, z]
                    there = list(here)
                    there[axis] = (there[axis] + step) % 4
                    pairs.append((role * 64 + chip_index(here), role * 64 + chip_index(there)))
    return pairs


def send(value, phase, step):
    return lax.ppermute(value, ("role", "shard"), shift_perm(phase, step))


def swap(value):
    return lax.ppermute(value, "role", [(0, 1), (1, 0)])


def plane_groups():
    groups = []
    for role in range(2):
        across, last = AXES[role][1], AXES[role][2]
        for fixed in range(4):
            group = []
            for z in range(4):
                for w in range(4):
                    coords = [0, 0, z]
                    coords[across], coords[last] = w, fixed
                    group.append(role * 64 + chip_index(coords))
            groups.append(group)
    return groups


def exchange(value):
    return lax.all_to_all(value, ("role", "shard"), 0, 0, axis_index_groups=plane_groups())


def ring(value, phase):
    return [value] + [send(value, phase, step) for step in (1, 2, 3)]


def after(value, *others):
    for other in others:
        cut = other[tuple(slice(0, min(n, m)) for n, m in zip(value.shape, other.shape))]
        zero = (cut * 0).astype(value.dtype)
        value = value + jnp.pad(zero, [(0, n - m) for n, m in zip(value.shape, zero.shape)])
    return value


def pick(table, index):
    hit = index[:, None] == jnp.arange(table.shape[0], dtype=jnp.int32)[None, :]
    return jnp.sum(jnp.where(hit, table[None, :], 0), axis=1)


def low_kernel(ids, x0, x1, x3, near_ref, far_ref, gain_ref, rows_ref, out_ref):
    gain = gain_ref[...].astype(F32)
    near = (near_ref[...].astype(F32) * gain).astype(BF)
    far = (far_ref[...].astype(F32) * gain).astype(BF)
    turn = (((1,), (1,)), ((), ()))
    parts = []
    for place, x in enumerate((x0, x1, x3)):
        block = x[...]
        rows = rows_ref[0:1, place * 128 : (place + 1) * 128]
        total = jnp.zeros((16, 128), F32)
        for base, table in ((0, near), (4, far)):
            if base == 4 and place > 0:
                continue
            got = lax.dot_general(table, block, turn, preferred_element_type=F32)
            for entry in range(4):
                total = total + jnp.where(rows == ids[base + entry], got[entry * 16 : (entry + 1) * 16, :], 0.0)
        parts.append(total)
    low = jnp.concatenate(parts, axis=1)
    for copy in range(16):
        out_ref[copy] = low


def make_low(ids, blocks, near, far, gain, rows):
    whole = pl.BlockSpec(memory_space=pltpu.VMEM)
    return pl.pallas_call(
        low_kernel,
        out_shape=jax.ShapeDtypeStruct((16, 16, 384), F32),
        in_specs=[pl.BlockSpec(memory_space=pltpu.SMEM)] + [whole] * 7,
        out_specs=whole,
        compiler_params=pltpu.CompilerParams(vmem_limit_bytes=48 * 1024 * 1024),
        cost_estimate=pl.CostEstimate(flops=2 * 256 * 128 * 4096, bytes_accessed=5 * 1024 * 1024, transcendentals=0),
    )(ids, *blocks, near, far, gain, rows)


def products_kernel(count, *refs):
    mine, others = refs[:count], refs[count : 2 * count]
    w_mine, w_other, pick_ref, own, other, own_sq, other_sq, base = refs[2 * count :]

    @pl.when(pl.program_id(0) == 0)
    def _():
        own[...] = jnp.zeros_like(own)
        other[...] = jnp.zeros_like(other)
        own_sq[...] = jnp.zeros_like(own_sq)
        other_sq[...] = jnp.zeros_like(other_sq)

    for parts, weights, out, square in ((mine, w_mine, own, own_sq), (others, w_other, other, other_sq)):
        x = jnp.concatenate([part[...] for part in parts], axis=0)
        out[...] += jnp.dot(x, weights[...], preferred_element_type=F32)
        wide = x.astype(F32)
        wide = wide * wide
        square[...] += sum(wide[:, i * 128 : (i + 1) * 128] for i in range(wide.shape[1] // 128))
        if out is own:
            base[...] = jnp.dot(pick_ref[...], x, preferred_element_type=F32)


def make_products(mine, others, weights, pick):
    step = 1024
    depth, width = weights.shape[0] // 2, weights.shape[1]
    count = len(mine)
    rows = 128 * count
    x_spec = pl.BlockSpec((128, step), lambda k: (0, k))
    mine_spec = pl.BlockSpec((step, width), lambda k: (k, 0))
    other_spec = pl.BlockSpec((step, width), lambda k: (k + depth // step, 0))
    fixed = lambda *shape: pl.BlockSpec(shape, lambda k: (0, 0))
    return pl.pallas_call(
        functools.partial(products_kernel, count),
        out_shape=[
            jax.ShapeDtypeStruct((rows, width), F32),
            jax.ShapeDtypeStruct((rows, width), F32),
            jax.ShapeDtypeStruct((rows, 128), F32),
            jax.ShapeDtypeStruct((rows, 128), F32),
            jax.ShapeDtypeStruct((8, depth), F32),
        ],
        grid=(depth // step,),
        in_specs=[x_spec] * (2 * count) + [mine_spec, other_spec, fixed(8, rows)],
        out_specs=[fixed(rows, width), fixed(rows, width), fixed(rows, 128), fixed(rows, 128), pl.BlockSpec((8, step), lambda k: (0, k))],
        compiler_params=pltpu.CompilerParams(vmem_limit_bytes=48 * 1024 * 1024),
        cost_estimate=pl.CostEstimate(
            flops=4 * rows * depth * width, bytes_accessed=(12 + 2 * count) * 1024 * 1024, transcendentals=0
        ),
    )(*mine, *others, weights, weights, pick)


def hidden_kernel(place, own_a, other_a, own_sq_a, other_sq_a, own_b, other_b, own_sq_b, other_sq_b, low_ref, low_other, ids_ref, pos_mine, pos_other, maps_ref, out_ref, out_other, low_got, sq, hidden, other, other_sq):
    def there(d, z, w):
        row = ((place[1] - w) & 3) * 128 + z * 32 + ((place[0] - d) & 3) * 8
        return pl.ds(pl.multiple_of(row, 8), 8)

    for part_a, part_b, into in ((other_a, other_b, other), (other_sq_a, other_sq_b, other_sq)):
        into[0:256, :] = part_a[0:256, :]
        into[256:384, :] = part_b[...]
        into[384:512, :] = part_a[256:384, :]
    source = lambda d: (d == 2, (0, 128, 0, 256)[d])
    fill = jnp.zeros((112, 512), F32)
    low_got[...] = jnp.concatenate([low_other[...], fill], axis=0).T
    low_mine = jnp.concatenate([low_ref[...], fill], axis=0).T
    parts = []
    for d in range(4):
        for z in range(4):
            for w in range(4):
                row = d * 128 + z * 32 + w * 8
                second, start = source(d)
                mine = (own_sq_b if second else own_sq_a)[start + z * 32 + w * 8 : start + z * 32 + w * 8 + 8, :]
                sq[row : row + 8, :] = mine + other_sq[there(d, z, w), :]
                parts.append(low_got[there(d, z, w), :])
    inv = lax.rsqrt(jnp.sum(sq[...], axis=1, keepdims=True) / 8192.0 + 1e-05)
    total = low_mine + jnp.concatenate(parts, axis=0)
    column = lax.broadcasted_iota(jnp.int32, (128, 128), 0)
    lane = lax.broadcasted_iota(jnp.int32, (128, 128), 1)
    spread = jnp.where(column == lane % 16, 1.0, 0.0).astype(BF)
    low = jnp.dot((total * inv).astype(BF), spread, preferred_element_type=F32)
    inv = jnp.broadcast_to(inv, (512, 128))
    lane = lax.broadcasted_iota(jnp.int32, (512, 128), 1)
    rest = ids_ref[...] - lane // 16
    acc = jnp.zeros(out_ref.shape, F32)
    for j in range(16):
        sides = [jnp.where(rest == 8 * (2 * j + i), low, 0.0).astype(BF) for i in range(2)]
        lhs = jnp.concatenate(sides, axis=1)
        acc = acc + jnp.dot(lhs, maps_ref[j * 256 : (j + 1) * 256, :], preferred_element_type=F32)
    width = out_ref.shape[1]
    for d in range(4):
        for z in range(4):
            for v in range(2):
                row = d * 128 + z * 32 + v * 16
                sums = [other[there(d, z, w), :] for w in (2 * v, 2 * v + 1)]
                second, start = source(d)
                start = start + z * 32 + v * 16
                both = (own_b if second else own_a)[start : start + 16, :] + jnp.concatenate(sums, axis=0)
                scale = jnp.concatenate([inv[row : row + 16, :]] * (width // 128), axis=1)
                gate = both[:, :width] * scale + 2.0 * acc[row : row + 16, :]
                up = both[:, width:] * scale
                hidden[row : row + 16, :] = (gate / (1.0 + jnp.exp(-gate)) * up).astype(BF)
    value = hidden[...]
    for pos_ref, out in ((pos_mine, out_ref), (pos_other, out_other)):
        pos = pos_ref[...]
        pick = jnp.concatenate([jnp.where(pos == lane + 128 * i, 1.0, 0.0).astype(BF) for i in range(4)], axis=1)
        out[...] = jnp.dot(pick, value, preferred_element_type=F32).astype(BF)


def make_hidden(place, first, second, low, low_other, ids, pos_mine, pos_other, maps):
    rows = 512
    width = maps.shape[1]
    whole = pl.BlockSpec(memory_space=pltpu.VMEM)
    return pl.pallas_call(
        hidden_kernel,
        out_shape=[jax.ShapeDtypeStruct((rows, width), BF)] * 2,
        in_specs=[pl.BlockSpec(memory_space=pltpu.SMEM)] + [whole] * 14,
        out_specs=[whole] * 2,
        scratch_shapes=[pltpu.VMEM((rows, 128), F32), pltpu.VMEM((rows, 128), F32), pltpu.VMEM((rows, width), BF), pltpu.VMEM((rows, 2 * width), F32), pltpu.VMEM((rows, 128), F32)],
        compiler_params=pltpu.CompilerParams(vmem_limit_bytes=48 * 1024 * 1024),
        cost_estimate=pl.CostEstimate(
            flops=2 * rows * 4096 * width, bytes_accessed=6 * 1024 * 1024, transcendentals=rows * width
        ),
    )(place, *first, *second, low, low_other, ids, pos_mine, pos_other, maps)


def down_kernel(mine_ref, other_ref, keep_ref, recv_ref, o0, o1, o2, o3):
    rows = jnp.concatenate([mine_ref[...], other_ref[...]], axis=1)
    weights = jnp.concatenate([keep_ref[...], recv_ref[...]], axis=0)
    total = jnp.dot(rows, weights, preferred_element_type=F32)
    for step, out in enumerate((o0, o1, o2, o3)):
        out[...] = total[step * 128 : (step + 1) * 128].astype(out.dtype)


def make_down(mine, other, keep, recv):
    rows, width = mine.shape
    columns = keep.shape[1]
    step = 1024
    whole = lambda x: pl.BlockSpec(x.shape, lambda i: (0, 0))
    tile = lambda n: pl.BlockSpec((n, step), lambda i: (0, i))
    return pl.pallas_call(
        down_kernel,
        out_shape=[jax.ShapeDtypeStruct((rows // 4, columns), F32 if d == 0 else BF) for d in range(4)],
        grid=(columns // step,),
        in_specs=[whole(mine), whole(other), tile(width), tile(width)],
        out_specs=[tile(rows // 4)] * 4,
        compiler_params=pltpu.CompilerParams(vmem_limit_bytes=48 * 1024 * 1024),
        cost_estimate=pl.CostEstimate(
            flops=4 * rows * width * columns, bytes_accessed=9 * 1024 * 1024, transcendentals=0
        ),
    )(mine, other, keep, recv)


def local(
    query,
    fresh_token_keys,
    fresh_token_values,
    stored_keys,
    stored_values,
    slot_cache_length,
    residual,
    prenorm_scale,
    request_cache_slot,
    request_adapter,
    gate_projection_levels,
    gate_group_scales,
    up_projection_levels,
    up_group_scales,
    down_projection_levels,
    down_group_scales,
    adapter_input_maps,
    adapter_gate_maps,
):
    role = lax.axis_index("role")
    shard = lax.axis_index("shard")
    here = (shard // 16, (shard // 4) % 4, shard % 4)
    half = residual.shape[1]
    units = gate_projection_levels.shape[1]
    first = role == 0

    def axis_of(mine, phase):
        a, b = AXES[0][phase], AXES[1][phase]
        return (a, b) if mine else (b, a)

    def by_role(pair, values):
        return jnp.where(first, values[pair[0]], values[pair[1]])

    def position(slot, mine):
        q = slot // 8
        chip = (q // 16, (q // 4) % 4, q % 4)
        last, across = axis_of(mine, 2), axis_of(mine, 1)
        total = (by_role(last, here) - by_role(last, chip)) % 4
        return (total * 16 + chip[2] * 4 + by_role(across, chip)) * 8 + slot % 8

    every = jnp.arange(512, dtype=jnp.int32)
    pos_of_request = position(request_cache_slot, True)
    hit_row = pos_of_request[None, :] == every[:, None]
    adapter_of_row = jnp.sum(jnp.where(hit_row, request_adapter[None, :], 0), axis=1)
    def request_slots(mine):
        z, w = (every // 32) % 4, (every // 8) % 4
        far = (by_role(axis_of(mine, 2), here) + every // 128) % 4
        swapped = first if mine else jnp.logical_not(first)
        chip = chip_index((jnp.where(swapped, far, w), jnp.where(swapped, w, far), z))
        lane = every % 8
        return pick(request_cache_slot, (lane // 4) * 256 + chip * 4 + lane % 4)

    slots = request_slots(True)
    pos_mine = jnp.broadcast_to(position(slots, True)[:, None], (512, 128))
    pos_other = jnp.broadcast_to(position(request_slots(False), True)[:, None], (512, 128))
    own_place = here[2] * 4 + by_role(axis_of(True, 1), here)
    own_pos = position(lax.dynamic_slice(slots, (own_place * 8,), (8,)), True)
    own_pick = (own_pos[:, None] == every[None, :]).astype(BF)

    gain = prenorm_scale.astype(F32)
    maps_raw = adapter_input_maps.reshape(-1, 2 * half)
    maps_keep = lax.dynamic_slice(maps_raw, (0, role * half), (maps_raw.shape[0], half))
    maps_send = lax.dynamic_slice(maps_raw, (0, (1 - role) * half), (maps_raw.shape[0], half))
    maps_near = jnp.concatenate([maps_keep, swap(maps_send)], axis=0)
    last = axis_of(True, 2)

    def adapters_at(step, of_role):
        mine = [jnp.where(first, last[0], last[1]) == axis for axis in range(3)]
        chip = chip_index([jnp.where(m, (c + step) % 4, c) for m, c in zip(mine, here)])
        return (of_role * 64 + chip) * 2 + jnp.arange(2, dtype=jnp.int32)

    ids = jnp.concatenate([adapters_at(step, of) for step in (0, 2) for of in (role, 1 - role)])

    attended = attend(
        query,
        fresh_token_keys,
        fresh_token_values,
        stored_keys,
        stored_values,
        slot_cache_length,
        stored_keys.shape[2] // HD,
        HD,
    )
    stream = (residual.astype(F32) + attended).astype(BF)

    weights, down_keep, down_send, token = make_weights(
        role,
        gate_projection_levels,
        gate_group_scales,
        up_projection_levels,
        up_group_scales,
        gain.reshape(1, -1),
        down_projection_levels,
        down_group_scales,
        stream[:, :128],
    )
    maps_far = send(after(maps_near, stream), 2, 2)

    plane = exchange(jnp.broadcast_to(stream[None], (16,) + stream.shape)).reshape(128, half)
    plane = after(plane, token, maps_far)
    down_recv = swap(down_send)

    up = send(plane, 2, 1)
    down = send(plane, 2, -1)
    far_block = send(up, 2, 1)
    blocks = (plane, up, far_block, down)
    gain_half = lax.dynamic_slice(gain, (role * half,), (half,)).reshape(1, half)
    low_rows = jnp.concatenate([adapter_of_row[:256], adapter_of_row[384:]]).reshape(1, 384)
    low = make_low(ids, (plane, up, down), maps_near, maps_far, gain_half, low_rows)
    low = jnp.sum(exchange(low), axis=0)
    others = [swap(block) for block in (plane, up, down)]
    pick_first = jnp.concatenate([own_pick[:, :256], own_pick[:, 384:]], axis=1)
    *early, base = make_products((plane, up, down), others, weights, after(pick_first, low))
    far_other = swap(after(far_block, early[0]))
    *late, base_far = make_products((far_block,), (far_other,), weights, own_pick[:, 256:384])
    got = ring(low, 2)
    column = {0: 0, 1: 128, 3: 256}
    sums = []
    for d in range(4):
        terms = [got[step][:, column[(d - step) % 4] :][:, :128] for step in range(4) if (d - step) % 4 != 2]
        sums.append(sum(terms[1:], terms[0]))
    low = jnp.concatenate(sums, axis=1)
    low_other = swap(low)

    ids_wide = jnp.broadcast_to(adapter_of_row[:, None], (512, 128))
    place = jnp.stack([by_role(axis_of(True, 2), here), by_role(axis_of(False, 2), here)])
    hidden, hidden_send = make_hidden(
        place, early, late, low, low_other, ids_wide, pos_mine, pos_other, adapter_gate_maps.reshape(-1, units)
    )
    hidden_other = swap(hidden_send)

    pieces = make_down(hidden, hidden_other, down_keep, down_recv)
    got = [send(pieces[step], 2, step) for step in (2, 1, 3)]
    total = pieces[0] + got[0].astype(F32) + got[1].astype(F32) + got[2].astype(F32)
    part = total.astype(BF).reshape(16, 8, half)
    total = jnp.sum(exchange(part).astype(F32), axis=0)
    result = (base + base_far + total).astype(BF)
    keep = lax.dynamic_slice(result, (role * 4, 0), (4, half))
    got = swap(lax.dynamic_slice(result, ((1 - role) * 4, 0), (4, half)))
    return jnp.concatenate([jnp.where(first, keep, got), jnp.where(first, got, keep)], axis=1)


def solution(mesh):
    return jax.shard_map(
        local,
        mesh=mesh,
        in_specs=(
            P("shard", "role"),
            P("shard", "role"),
            P("shard", "role"),
            P("shard", None, "role"),
            P("shard", None, "role"),
            P("shard"),
            P("shard", "role"),
            P(),
            P(),
            P(),
            P(None, ("role", "shard")),
            P(None, ("role", "shard")),
            P(None, ("role", "shard")),
            P(None, ("role", "shard")),
            P(("role", "shard"), None),
            P(("role", "shard"), None),
            P(("role", "shard"), None, None),
            P(None, None, ("role", "shard")),
        ),
        out_specs=P(("role", "shard"), None),
        check_vma=False,
    )
```

time: 502 us -> 162 us (0.32); the launches traced: 493 us -> 161 us
  waiting for transfers between devices: 271 us -> 63.7 us
  blocking collectives: 68.9 us -> 0 us
  local copies, waits for them, and re-layouts: 54.8 us -> 4.07 us
  starting transfers between devices: 0.08 us -> 42.7 us
  matrix products: 46.6 us -> 5.41 us
  Pallas kernels: 0 us -> 36.3 us
  other arithmetic: 37.4 us -> 7.99 us
  between operations: 13.9 us -> 0.63 us
    unnamed x3 -> x0, waiting for transfers between devices: 208 us -> none
    psum x1 -> x0, blocking collectives: 65.8 us -> none  [local(): low = lax.psum(low_part, ('role', 'shard')).astype(jnp.bfloat16)]
    all_gather x1 -> x0, waiting for transfers between devices: 62.7 us -> none  [local(): whole = lax.all_gather(joined, 'shard', axis=0, tiled=True)]
    gather x7 -> x0, local copies, waits for them, and re-layouts: 54.6 us -> none  [the longest x1 20.4 us: local(): sorted_entries = jnp.take(normed, request_cache_slot, axis=0)]
    dot_general x7 -> x3, matrix products: 46.6 us -> 5.41 us  [the longest x1 3.65 us: attend(): jnp.einsum('skgd,slkd->skgl', queries, keys, preferred_element_type=F32)]
    ppermute x0 -> x19, waiting for transfers between devices: none -> 41.1 us  [the longest x10 38.7 us: send(): return lax.ppermute(value, ('role', 'shard'), shift_perm(phase, step))]
    pallas_call x0 -> x6, Pallas kernels: none -> 36.3 us  [the longest x2 13 us: make_products(): pl.pallas_call(functools.partial(products_kernel, count), out_shape=[jax....]
    ppermute x0 -> x19, starting transfers between devices: none -> 25.3 us  [the longest x9 15.1 us: swap(): return lax.ppermute(value, 'role', [(0, 1), (1, 0)])]
  transfers between devices with their start and end apart: 2 -> 22, of which waited for: 2 -> 11; matrix products, arithmetic and copies ran while one was open for 5% -> 7% of each run, Pallas kernels for 0% -> 20%
where the time goes in v2:
time: 162 us; the launch traced here: 161 us
  waiting for transfers between devices  63.7 us (39%)
  starting transfers between devices  42.7 us (26%)
  Pallas kernels  36.3 us (22%)
  other arithmetic  7.99 us (5%)
  matrix products  5.41 us (3%)
  local copies, waits for them, and re-layouts  4.07 us (3%)
    ppermute x10, waiting for transfers between devices, send(): return lax.ppermute(value, ('role', 'shard'), shift_perm(phase, step))  38.7 us
    all_to_all x3, waiting for transfers between devices, exchange(): lax.all_to_all(value, ('role', 'shard'), 0, 0, axis_index_groups=plane_gr...  22.6 us
    all_to_all x3, starting transfers between devices, exchange(): lax.all_to_all(value, ('role', 'shard'), 0, 0, axis_index_groups=plane_gr...  17.4 us
    ppermute x9, starting transfers between devices, swap(): return lax.ppermute(value, 'role', [(0, 1), (1, 0)])  15.1 us
    pallas_call x2, Pallas kernels, make_products(): pl.pallas_call(functools.partial(products_kernel, count), out_shape=[jax....  13 us
    pallas_call x1, Pallas kernels, make_weights(): pl.pallas_call(weights_kernel, out_shape=[jax.ShapeDtypeStruct((depth, 2...  11.7 us
    ppermute x10, starting transfers between devices, send(): return lax.ppermute(value, ('role', 'shard'), shift_perm(phase, step))  10.2 us
    pallas_call x1, Pallas kernels, make_down(): pl.pallas_call(down_kernel, out_shape=[jax.ShapeDtypeStruct((rows // 4, c...  4.87 us
  transfers between devices with their start and end apart: 22, of which 11 were waited for; matrix products, arithmetic and copies ran while one was open for 7% of the time, Pallas kernels for 20%

profile of v2, /device:TPU:1, one launch (start us, length us, event | category | flops | bytes accessed | tf_op | source)
XLA Modules:
  0.0 160.8 jit_solution(7231326911311123930)
XLA Ops:
  1.1 1.5 collective-permute-start
  4.3 3.6 %fusion.91 = (f32[8,2,16]{2,1,0:T(2,128)S(1)}, f32[8,2,16,1024]{3,2,1,0:T(8,128)S(1)}) fusion(bf16[8,2,16,128]{3,0,2,1:T(8,128)(2,1)} %bitcast.60, pred[8,1024]{1,0:T(8,128)(4,1)S(1)} %iota_compare_fusion.3, bf16[8,1024,256]{2,1,0:T(8,128)(2,1)} %param.21), kind=kOutput, calls=%fused_computation.244 | convolution fusion | flops 67895040 | bytes 5317632 | tf_op jit(solution)/shard_map/skgd,slkd->skgl/dot_general | solution.py:35
  9.5 3.1 %collective-permute-start.1 = (bf16[64,4096]{1,0:T(8,128)(2,1)S(1)}, bf16[64,4096]{1,0:T(8,128)(2,1)S(1)}, u32[]{:S(2)}, u32[]{:S(2)}) collective-permute-start(bf16[64,4096]{1,0:T(8,128)(2,1)S(1)} %get-tuple-element.50), channel_id=1, source_target_pairs={{0,32},{1,33},{2,34},{3,35},{4,36},{5,37},{6,38},{7,39},{8,40},{9,... | collective-permute-start | bytes 1572872 | tf_op jit(solution)/shard_map/ppermute | solution.py:132
  13.7 7.6 %all-to-all-start = ((bf16[16,8,4096]{2,1,0:T(8,128)(2,1)}), bf16[16,8,4096]{2,1,0:T(8,128)(2,1)S(1)}, u32[]{:S(2)}, u32[]{:S(2)}) async-start(bf16[16,8,4096]{2,1,0:T(8,128)(2,1)} %broadcast_in_dim.44), calls=%async_computation | async-start | bytes 2097152 | tf_op jit(solution)/shard_map/all_to_all | solution.py:155
  21.3 11.7 %shard_map.172 = (bf16[8192,512]{1,0:T(8,128)(2,1)}, bf16[256,4096]{1,0:T(8,128)(2,1)S(1)}, bf16[256,4096]{1,0:T(8,128)(2,1)}, bf16[16,128]{1,0:T(8,128)(2,1)S(1)}) custom-call(s32[1]{0:T(128)} %bitcast.7.role, bf16[8192,256]{1,0:T(8,128)(2,1)} %gate_ref.1, f32[64,256]{1,0:T(8,128)S(1)} %copy-done.3, bf16[8192,256]{1,0:T(8,128)(2,1)} %up_ref.1, ...), custom_call_target="tpu_custom_call" | custom-call | flops 25165824 | bytes 25165824 | tf_op jit(solution)/shard_map/pallas_call | solution.py:89
  40.5 2.0 %collective-permute-start.14 = (bf16[256,4096]{1,0:T(8,128)(2,1)}, bf16[256,4096]{1,0:T(8,128)(2,1)}, u32[]{:S(2)}, u32[]{:S(2)}) collective-permute-start(bf16[256,4096]{1,0:T(8,128)(2,1)} %get-tuple-element.40), channel_id=1, source_target_pairs={{0,64},{64,0},{1,65},{65,1},{2,66},{66,2},{3,67},{67,3},{4,68},{68... | collective-permute-start | bytes 6291464 | tf_op jit(solution)/shard_map/ppermute | solution.py:136
  43.3 9.6 %collective-permute-done.2.x1.refs_1_ = bf16[128,4096]{1,0:T(8,128)(2,1)S(1)} collective-permute-done((bf16[128,4096]{1,0:T(8,128)(2,1)S(1)}, bf16[128,4096]{1,0:T(8,128)(2,1)S(1)}, u32[]{:S(2)}, u32[]{:S(2)}) %collective-permute-start.2) | collective-permute-done | bytes 1048608 | tf_op jit(solution)/shard_map/ppermute | solution.py:132
  52.9 2.2 %collective-permute-start.5 = (bf16[128,4096]{1,0:T(8,128)(2,1)S(1)}, bf16[128,4096]{1,0:T(8,128)(2,1)}, u32[]{:S(2)}, u32[]{:S(2)}) collective-permute-start(bf16[128,4096]{1,0:T(8,128)(2,1)S(1)} %collective-permute-done.2.x1.refs_1_), channel_id=1, source_target_pairs={{0,64},{64,0},{1,65},{65,1},{2,66},{66,2},{3,67},{67,3},{4,68},{68... | collective-permute-start | bytes 3145736 | tf_op jit(solution)/shard_map/ppermute | solution.py:136
  55.9 3.5 %shard_map.173 = f32[16,16,384]{2,1,0:T(8,128)} custom-call(s32[8]{0:T(128)S(1)} %pad_add_fusion.3.ids, bf16[128,4096]{1,0:T(8,128)(2,1)S(1)} %fusion.19.x0.refs_0_, bf16[128,4096]{1,0:T(8,128)(2,1)S(1)} %collective-permute-done.2.x1.refs_1_, bf16[128,4096]{1,0:T(8,128)(2,1)} %collective-permute-done.3.x3.refs_2_, ...), custom_call_target="tpu_custom_call" | custom-call | flops 268435456 | bytes 5242880 | tf_op jit(solution)/shard_map/pallas_call | solution.py:199
  59.5 4.9 %all-to-all-start.1 = ((f32[16,16,384]{2,1,0:T(8,128)}), f32[16,16,384]{2,1,0:T(8,128)}, u32[]{:S(2)}, u32[]{:S(2)}) async-start(f32[16,16,384]{2,1,0:T(8,128)} %shard_map.173), calls=%async_computation.1 | async-start | bytes 786432 | tf_op jit(solution)/shard_map/all_to_all | solution.py:155
  65.7 7.3 %all-to-all-done.1 = f32[16,16,384]{2,1,0:T(8,128)} async-done(((f32[16,16,384]{2,1,0:T(8,128)}), f32[16,16,384]{2,1,0:T(8,128)}, u32[]{:S(2)}, u32[]{:S(2)}) %all-to-all-start.1) | async-done | bytes 393248 | tf_op jit(solution)/shard_map/all_to_all | solution.py:155
  74.1 7.7 %shard_map.174 = (f32[384,512]{1,0:T(8,128)S(1)}, f32[384,512]{1,0:T(8,128)S(1)}, f32[384,128]{1,0:T(8,128)S(1)}, f32[384,128]{1,0:T(8,128)S(1)}, f32[8,4096]{1,0:T(8,128)S(1)}) custom-call(bf16[128,4096]{1,0:T(8,128)(2,1)S(1)} %fusion.19.x0.refs_0_, bf16[128,4096]{1,0:T(8,128)(2,1)S(1)} %collective-permute-done.2.x1.refs_1_, ...), custom_call_target="tpu_custom_call" | custom-call | flops 3221225472 | bytes 18874368 | tf_op jit(solution)/shard_map/pallas_call | solution.py:239
  82.0 3.4 %collective-permute-start.8 = (bf16[128,4096]{1,0:T(8,128)(2,1)S(1)}, bf16[128,4096]{1,0:T(8,128)(2,1)S(1)}, u32[]{:S(2)}, u32[]{:S(2)}) collective-permute-start(bf16[128,4096]{1,0:T(8,128)(2,1)S(1)} %pad_add_fusion), channel_id=1, source_target_pairs={{0,64},{64,0},{1,65},{65,1},{2,66},{66,2},{3,67},{67,3},{4,68},{68... | collective-permute-start | bytes 3145736 | tf_op jit(solution)/shard_map/ppermute | solution.py:136
  89.5 1.7 %collective-permute-done.11 = f32[16,384]{1,0:T(8,128)S(1)} collective-permute-done((f32[16,384]{1,0:T(8,128)S(1)}, f32[16,384]{1,0:T(8,128)S(1)}, u32[]{:S(2)}, u32[]{:S(2)}) %collective-permute-start.11) | collective-permute-done | bytes 24608 | tf_op jit(solution)/shard_map/ppermute | solution.py:132
  91.2 2.7 %collective-permute-start.12 = (f32[16,512]{1,0:T(8,128)S(1)}, f32[16,512]{1,0:T(8,128)S(1)}, u32[]{:S(2)}, u32[]{:S(2)}) collective-permute-start(f32[16,512]{1,0:T(8,128)S(1)} %pad_maximum_fusion.2.low_ref), channel_id=1, source_target_pairs={{0,64},{64,0},{1,65},{65,1},{2,66},{66,2},{3,67},{67,3},{4,68},{68... | collective-permute-start | bytes 98312 | tf_op jit(solution)/shard_map/ppermute | solution.py:136
  93.9 5.2 %shard_map.175 = (f32[128,512]{1,0:T(8,128)S(1)}, f32[128,512]{1,0:T(8,128)S(1)}, f32[128,128]{1,0:T(8,128)S(1)}, f32[128,128]{1,0:T(8,128)S(1)}, f32[8,4096]{1,0:T(8,128)S(1)}) custom-call(bf16[128,4096]{1,0:T(8,128)(2,1)S(1)} %collective-permute-done.7.refs_0_, bf16[128,4096]{1,0:T(8,128)(2,1)S(1)} %collective-permute-done.8.refs_1_, ...), custom_call_target="tpu_custom_call" | custom-call | flops 1073741824 | bytes 14680064 | tf_op jit(solution)/shard_map/pallas_call | solution.py:239
  99.6 3.1 %shard_map.176 = (bf16[512,256]{1,0:T(8,128)(2,1)S(1)}, bf16[512,256]{1,0:T(8,128)(2,1)S(1)}) custom-call(s32[2]{0:T(128)S(1)} %pad_add_fusion.4.place, f32[384,512]{1,0:T(8,128)S(1)} %get-tuple-element.28.own_a, f32[384,512]{1,0:T(8,128)S(1)} %get-tuple-element.30.other_a, f32[384,128]{1,0:T(8,128)S(1)} %get-tuple-element.31.own_sq_a, ...), custom_call_target="tpu_custom_call" | custom-call | flops 1073741824 | bytes 6291456 | tf_op jit(solution)/shard_map/pallas_call | solution.py:318
  104.3 4.9 %shard_map.177 = (f32[128,4096]{1,0:T(8,128)S(1)}, bf16[128,4096]{1,0:T(8,128)(2,1)S(1)}, bf16[128,4096]{1,0:T(8,128)(2,1)S(1)}, bf16[128,4096]{1,0:T(8,128)(2,1)S(1)}) custom-call(bf16[512,256]{1,0:T(8,128)(2,1)S(1)} %get-tuple-element.37.mine_ref, bf16[512,256]{1,0:T(8,128)(2,1)S(1)} %collective-permute-done.13.other_ref, bf16[256,4096]{1,0:T(8,128)(2,1)} %copy-done.6, ...), custom_call_target="tpu_custom_call" | custom-call | flops 2147483648 | bytes 9437184 | tf_op jit(solution)/shard_map/pallas_call | solution.py:345
  110.8 12.5 %collective-permute-done.17 = bf16[128,4096]{1,0:T(8,128)(2,1)S(1)} collective-permute-done((bf16[128,4096]{1,0:T(8,128)(2,1)S(1)}, bf16[128,4096]{1,0:T(8,128)(2,1)S(1)}, u32[]{:S(2)}, u32[]{:S(2)}) %collective-permute-start.17) | collective-permute-done | bytes 1048608 | tf_op jit(solution)/shard_map/ppermute | solution.py:132
  123.2 12.5 %collective-permute-done.16 = bf16[128,4096]{1,0:T(8,128)(2,1)S(1)} collective-permute-done((bf16[128,4096]{1,0:T(8,128)(2,1)S(1)}, bf16[128,4096]{1,0:T(8,128)(2,1)S(1)}, u32[]{:S(2)}, u32[]{:S(2)}) %collective-permute-start.16) | collective-permute-done | bytes 1048608 | tf_op jit(solution)/shard_map/ppermute | solution.py:132
  135.8 1.6 fusion.18
  137.3 4.9 %all-to-all-start.2 = ((bf16[16,8,4096]{2,1,0:T(8,128)(2,1)}), bf16[16,8,4096]{2,1,0:T(8,128)(2,1)S(1)}, u32[]{:S(2)}, u32[]{:S(2)}) async-start(bf16[16,8,4096]{2,1,0:T(8,128)(2,1)} %fusion.18), calls=%async_computation.2 | async-start | bytes 2097152 | tf_op jit(solution)/shard_map/all_to_all | solution.py:155
  142.3 14.0 %all-to-all-done.2 = bf16[16,8,4096]{2,1,0:T(8,128)(2,1)S(1)} async-done(((bf16[16,8,4096]{2,1,0:T(8,128)(2,1)}), bf16[16,8,4096]{2,1,0:T(8,128)(2,1)S(1)}, u32[]{:S(2)}, u32[]{:S(2)}) %all-to-all-start.2) | async-done | bytes 1048608 | tf_op jit(solution)/shard_map/all_to_all | solution.py:155
  156.5 2.7 %collective-permute-start.18 = (bf16[4,4096]{1,0:T(4,128)(2,1)S(1)}, bf16[4,4096]{1,0:T(4,128)(2,1)S(1)}, u32[]{:S(2)}, u32[]{:S(2)}) collective-permute-start(bf16[4,4096]{1,0:T(4,128)(2,1)S(1)} %constant_dynamic-slice_fusion), channel_id=1, source_target_pairs={{0,64},{64,0},{1,65},{65,1},{2,66},{66,2},{3,67},{67,3},{4,68},{68... | collective-permute-start | bytes 98312 | tf_op jit(solution)/shard_map/ppermute | solution.py:136
  (104 shorter events, 25.9 us)
Async XLA Ops:
  1.1 8.2 %collective-permute-start = (bf16[32,4096]{1,0:T(8,128)(2,1)S(1)}, bf16[32,4096]{1,0:T(8,128)(2,1)S(1)}, u32[]{:S(2)}, u32[]{:S(2)}) collective-permute-start(bf16[32,4096]{1,0:T(8,128)(2,1)S(1)} %get-tuple-element.52), channel_id=1, source_target_pairs={{0,64},{64,0},{1,65},{65,1},{2,66},{66,2},{3,67},{67,3},{4,68},{68... | collective-permute-start | bytes 786440 | tf_op jit(solution)/shard_map/ppermute | solution.py:136
  9.3 12.0 %copy-start.3 = (f32[64,256]{1,0:T(8,128)S(1)}, f32[64,256]{1,0:T(8,128)}, u32[]{:S(2)}) copy-start(f32[64,256]{1,0:T(8,128)} %gate_scale.1) | copy-start | bytes 196612
  9.5 25.0 %collective-permute-start.1 = (bf16[64,4096]{1,0:T(8,128)(2,1)S(1)}, bf16[64,4096]{1,0:T(8,128)(2,1)S(1)}, u32[]{:S(2)}, u32[]{:S(2)}) collective-permute-start(bf16[64,4096]{1,0:T(8,128)(2,1)S(1)} %get-tuple-element.50), channel_id=1, source_target_pairs={{0,32},{1,33},{2,34},{3,35},{4,36},{5,37},{6,38},{7,39},{8,40},{9,... | collective-permute-start | bytes 1572872 | tf_op jit(solution)/shard_map/ppermute | solution.py:132
  13.7 22.9 %all-to-all-start = ((bf16[16,8,4096]{2,1,0:T(8,128)(2,1)}), bf16[16,8,4096]{2,1,0:T(8,128)(2,1)S(1)}, u32[]{:S(2)}, u32[]{:S(2)}) async-start(bf16[16,8,4096]{2,1,0:T(8,128)(2,1)} %broadcast_in_dim.44), calls=%async_computation | async-start | bytes 2097152 | tf_op jit(solution)/shard_map/all_to_all | solution.py:155
  37.7 15.2 %collective-permute-start.2 = (bf16[128,4096]{1,0:T(8,128)(2,1)S(1)}, bf16[128,4096]{1,0:T(8,128)(2,1)S(1)}, u32[]{:S(2)}, u32[]{:S(2)}) collective-permute-start(bf16[128,4096]{1,0:T(8,128)(2,1)S(1)} %fusion.19.x0.refs_0_), channel_id=1, source_target_pairs={{0,16},{1,17},{2,18},{3,19},{4,20},{5,21},{6,22},{7,23},{8,24},{9,... | collective-permute-start | bytes 3145736 | tf_op jit(solution)/shard_map/ppermute | solution.py:132
  39.1 16.1 %collective-permute-start.3 = (bf16[128,4096]{1,0:T(8,128)(2,1)S(1)}, bf16[128,4096]{1,0:T(8,128)(2,1)}, u32[]{:S(2)}, u32[]{:S(2)}) collective-permute-start(bf16[128,4096]{1,0:T(8,128)(2,1)S(1)} %fusion.19.x0.refs_0_), channel_id=1, source_target_pairs={{0,48},{1,49},{2,50},{3,51},{4,52},{5,53},{6,54},{7,55},{8,56},{9,... | collective-permute-start | bytes 3145736 | tf_op jit(solution)/shard_map/ppermute | solution.py:132
  40.5 62.4 %collective-permute-start.14 = (bf16[256,4096]{1,0:T(8,128)(2,1)}, bf16[256,4096]{1,0:T(8,128)(2,1)}, u32[]{:S(2)}, u32[]{:S(2)}) collective-permute-start(bf16[256,4096]{1,0:T(8,128)(2,1)} %get-tuple-element.40), channel_id=1, source_target_pairs={{0,64},{64,0},{1,65},{65,1},{2,66},{66,2},{3,67},{67,3},{4,68},{68... | collective-permute-start | bytes 6291464 | tf_op jit(solution)/shard_map/ppermute | solution.py:136
  43.2 30.9 %collective-permute-start.4 = (bf16[128,4096]{1,0:T(8,128)(2,1)S(1)}, bf16[128,4096]{1,0:T(8,128)(2,1)}, u32[]{:S(2)}, u32[]{:S(2)}) collective-permute-start(bf16[128,4096]{1,0:T(8,128)(2,1)S(1)} %fusion.19.x0.refs_0_), channel_id=1, source_target_pairs={{0,64},{64,0},{1,65},{65,1},{2,66},{66,2},{3,67},{67,3},{4,68},{68... | collective-permute-start | bytes 3145736 | tf_op jit(solution)/shard_map/ppermute | solution.py:136
  52.9 21.2 %collective-permute-start.5 = (bf16[128,4096]{1,0:T(8,128)(2,1)S(1)}, bf16[128,4096]{1,0:T(8,128)(2,1)}, u32[]{:S(2)}, u32[]{:S(2)}) collective-permute-start(bf16[128,4096]{1,0:T(8,128)(2,1)S(1)} %collective-permute-done.2.x1.refs_1_), channel_id=1, source_target_pairs={{0,64},{64,0},{1,65},{65,1},{2,66},{66,2},{3,67},{67,3},{4,68},{68... | collective-permute-start | bytes 3145736 | tf_op jit(solution)/shard_map/ppermute | solution.py:136
  55.2 18.9 %collective-permute-start.6 = (bf16[128,4096]{1,0:T(8,128)(2,1)}, bf16[128,4096]{1,0:T(8,128)(2,1)}, u32[]{:S(2)}, u32[]{:S(2)}) collective-permute-start(bf16[128,4096]{1,0:T(8,128)(2,1)} %collective-permute-done.3.x3.refs_2_), channel_id=1, source_target_pairs={{0,64},{64,0},{1,65},{65,1},{2,66},{66,2},{3,67},{67,3},{4,68},{68... | collective-permute-start | bytes 3145736 | tf_op jit(solution)/shard_map/ppermute | solution.py:136
  59.5 13.6 %all-to-all-start.1 = ((f32[16,16,384]{2,1,0:T(8,128)}), f32[16,16,384]{2,1,0:T(8,128)}, u32[]{:S(2)}, u32[]{:S(2)}) async-start(f32[16,16,384]{2,1,0:T(8,128)} %shard_map.173), calls=%async_computation.1 | async-start | bytes 786432 | tf_op jit(solution)/shard_map/all_to_all | solution.py:155
  64.4 17.5 %collective-permute-start.7 = (bf16[128,4096]{1,0:T(8,128)(2,1)S(1)}, bf16[128,4096]{1,0:T(8,128)(2,1)S(1)}, u32[]{:S(2)}, u32[]{:S(2)}) collective-permute-start(bf16[128,4096]{1,0:T(8,128)(2,1)S(1)} %collective-permute-done.2.x1.refs_1_), channel_id=1, source_target_pairs={{0,16},{1,17},{2,18},{3,19},{4,20},{5,21},{6,22},{7,23},{8,24},{9,... | collective-permute-start | bytes 3145736 | tf_op jit(solution)/shard_map/ppermute | solution.py:132
  82.0 11.9 %collective-permute-start.8 = (bf16[128,4096]{1,0:T(8,128)(2,1)S(1)}, bf16[128,4096]{1,0:T(8,128)(2,1)S(1)}, u32[]{:S(2)}, u32[]{:S(2)}) collective-permute-start(bf16[128,4096]{1,0:T(8,128)(2,1)S(1)} %pad_add_fusion), channel_id=1, source_target_pairs={{0,64},{64,0},{1,65},{65,1},{2,66},{66,2},{3,67},{67,3},{4,68},{68... | collective-permute-start | bytes 3145736 | tf_op jit(solution)/shard_map/ppermute | solution.py:136
  85.5 2.7 %collective-permute-start.10 = (f32[16,384]{1,0:T(8,128)S(1)}, f32[16,384]{1,0:T(8,128)S(1)}, u32[]{:S(2)}, u32[]{:S(2)}) collective-permute-start(f32[16,384]{1,0:T(8,128)S(1)} %reduce_sum.57), channel_id=1, source_target_pairs={{0,48},{1,49},{2,50},{3,51},{4,52},{5,53},{6,54},{7,55},{8,56},{9,... | collective-permute-start | bytes 73736 | tf_op jit(solution)/shard_map/ppermute | solution.py:132
  85.6 4.0 %collective-permute-start.9 = (f32[16,384]{1,0:T(8,128)S(1)}, f32[16,384]{1,0:T(8,128)S(1)}, u32[]{:S(2)}, u32[]{:S(2)}) collective-permute-start(f32[16,384]{1,0:T(8,128)S(1)} %reduce_sum.57), channel_id=1, source_target_pairs={{0,16},{1,17},{2,18},{3,19},{4,20},{5,21},{6,22},{7,23},{8,24},{9,... | collective-permute-start | bytes 73736 | tf_op jit(solution)/shard_map/ppermute | solution.py:132
  87.0 4.2 %collective-permute-start.11 = (f32[16,384]{1,0:T(8,128)S(1)}, f32[16,384]{1,0:T(8,128)S(1)}, u32[]{:S(2)}, u32[]{:S(2)}) collective-permute-start(f32[16,384]{1,0:T(8,128)S(1)} %reduce_sum.57), channel_id=1, source_target_pairs={{0,32},{1,33},{2,34},{3,35},{4,36},{5,37},{6,38},{7,39},{8,40},{9,... | collective-permute-start | bytes 73736 | tf_op jit(solution)/shard_map/ppermute | solution.py:132
  91.2 8.0 %collective-permute-start.12 = (f32[16,512]{1,0:T(8,128)S(1)}, f32[16,512]{1,0:T(8,128)S(1)}, u32[]{:S(2)}, u32[]{:S(2)}) collective-permute-start(f32[16,512]{1,0:T(8,128)S(1)} %pad_maximum_fusion.2.low_ref), channel_id=1, source_target_pairs={{0,64},{64,0},{1,65},{65,1},{2,66},{66,2},{3,67},{67,3},{4,68},{68... | collective-permute-start | bytes 98312 | tf_op jit(solution)/shard_map/ppermute | solution.py:136
  102.7 1.6 %collective-permute-start.13 = (bf16[512,256]{1,0:T(8,128)(2,1)S(1)}, bf16[512,256]{1,0:T(8,128)(2,1)S(1)}, u32[]{:S(2)}, u32[]{:S(2)}) collective-permute-start(bf16[512,256]{1,0:T(8,128)(2,1)S(1)} %get-tuple-element.38), channel_id=1, source_target_pairs={{0,64},{64,0},{1,65},{65,1},{2,66},{66,2},{3,67},{67,3},{4,68},{68... | collective-permute-start | bytes 786440 | tf_op jit(solution)/shard_map/ppermute | solution.py:136
  109.2 14.0 %collective-permute-start.17 = (bf16[128,4096]{1,0:T(8,128)(2,1)S(1)}, bf16[128,4096]{1,0:T(8,128)(2,1)S(1)}, u32[]{:S(2)}, u32[]{:S(2)}) collective-permute-start(bf16[128,4096]{1,0:T(8,128)(2,1)S(1)} %get-tuple-element.44), channel_id=1, source_target_pairs={{0,48},{1,49},{2,50},{3,51},{4,52},{5,53},{6,54},{7,55},{8,56},{9,... | collective-permute-start | bytes 3145736 | tf_op jit(solution)/shard_map/ppermute | solution.py:132
  109.3 26.5 %collective-permute-start.16 = (bf16[128,4096]{1,0:T(8,128)(2,1)S(1)}, bf16[128,4096]{1,0:T(8,128)(2,1)S(1)}, u32[]{:S(2)}, u32[]{:S(2)}) collective-permute-start(bf16[128,4096]{1,0:T(8,128)(2,1)S(1)} %get-tuple-element.43), channel_id=1, source_target_pairs={{0,16},{1,17},{2,18},{3,19},{4,20},{5,21},{6,22},{7,23},{8,24},{9,... | collective-permute-start | bytes 3145736 | tf_op jit(solution)/shard_map/ppermute | solution.py:132
  110.8 25.0 %collective-permute-start.15 = (bf16[128,4096]{1,0:T(8,128)(2,1)S(1)}, bf16[128,4096]{1,0:T(8,128)(2,1)S(1)}, u32[]{:S(2)}, u32[]{:S(2)}) collective-permute-start(bf16[128,4096]{1,0:T(8,128)(2,1)S(1)} %get-tuple-element.42), channel_id=1, source_target_pairs={{0,32},{1,33},{2,34},{3,35},{4,36},{5,37},{6,38},{7,39},{8,40},{9,... | collective-permute-start | bytes 3145736 | tf_op jit(solution)/shard_map/ppermute | solution.py:132
  135.8 25.0 %copy-start.1 = (bf16[8,256]{1,0:T(8,128)(2,1)S(1)}, bf16[8,256]{1,0:T(8,128)(2,1)}, u32[]{:S(2)}) copy-start(bf16[8,256]{1,0:T(8,128)(2,1)} %param.19) | copy-start | bytes 12292
  137.3 19.0 %all-to-all-start.2 = ((bf16[16,8,4096]{2,1,0:T(8,128)(2,1)}), bf16[16,8,4096]{2,1,0:T(8,128)(2,1)S(1)}, u32[]{:S(2)}, u32[]{:S(2)}) async-start(bf16[16,8,4096]{2,1,0:T(8,128)(2,1)} %fusion.18), calls=%async_computation.2 | async-start | bytes 2097152 | tf_op jit(solution)/shard_map/all_to_all | solution.py:155
  156.5 3.6 %collective-permute-start.18 = (bf16[4,4096]{1,0:T(4,128)(2,1)S(1)}, bf16[4,4096]{1,0:T(4,128)(2,1)S(1)}, u32[]{:S(2)}, u32[]{:S(2)}) collective-permute-start(bf16[4,4096]{1,0:T(4,128)(2,1)S(1)} %constant_dynamic-slice_fusion), channel_id=1, source_target_pairs={{0,64},{64,0},{1,65},{65,1},{2,66},{66,2},{3,67},{67,3},{4,68},{68... | collective-permute-start | bytes 98312 | tf_op jit(solution)/shard_map/ppermute | solution.py:136
  (11 other events, 71.2 us)

commit v3 on v2

--- a/solution.py
+++ b/solution.py
@@ -465,11 +465,11 @@
     gain_half = lax.dynamic_slice(gain, (role * half,), (half,)).reshape(1, half)
     low_rows = jnp.concatenate([adapter_of_row[:256], adapter_of_row[384:]]).reshape(1, 384)
     low = make_low(ids, (plane, up, down), maps_near, maps_far, gain_half, low_rows)
-    low = jnp.sum(exchange(low), axis=0)
     others = [swap(block) for block in (plane, up, down)]
     pick_first = jnp.concatenate([own_pick[:, :256], own_pick[:, 384:]], axis=1)
-    *early, base = make_products((plane, up, down), others, weights, after(pick_first, low))
-    far_other = swap(after(far_block, early[0]))
+    *early, base = make_products((plane, up, down), others, weights, after(pick_first, low[0]))
+    low = jnp.sum(after(exchange(low), early[0][None]), axis=0)
+    far_other = swap(after(far_block, low))
     *late, base_far = make_products((far_block,), (far_other,), weights, own_pick[:, 256:384])
     got = ring(low, 2)
     column = {0: 0, 1: 128, 3: 256}

time: 162 us -> 160 us (0.988)
  waiting for transfers between devices: 63.7 us -> 57.6 us
  local copies, waits for them, and re-layouts: 4.07 us -> 6.52 us
    all_to_all x3, waiting for transfers between devices: 22.6 us -> 15.3 us  [exchange(): lax.all_to_all(value, ('role', 'shard'), 0, 0, axis_index_groups=plane_gr...]
    ppermute x10, starting transfers between devices: 10.2 us -> 14.8 us  [send(): return lax.ppermute(value, ('role', 'shard'), shift_perm(phase, step))]
    ppermute x9, starting transfers between devices: 15.1 us -> 11 us  [swap(): return lax.ppermute(value, 'role', [(0, 1), (1, 0)])]
    unnamed x26 -> x38, local copies, waits for them, and re-layouts: 1.46 us -> 3.94 us
  transfers between devices with their start and end apart: 22 -> 22, of which waited for: 11 -> 10; matrix products, arithmetic and copies ran while one was open for 7% -> 7% of each run, Pallas kernels for 20% -> 20%
where the time goes in v3:
time: 160 us; the launch traced here: 159 us
  waiting for transfers between devices  57.6 us (36%)
  starting transfers between devices  43.7 us (27%)
  Pallas kernels  36.2 us (23%)
  other arithmetic  8.63 us (5%)
  local copies, waits for them, and re-layouts  6.52 us (4%)
  matrix products  5.41 us (3%)
    ppermute x10, waiting for transfers between devices, send(): return lax.ppermute(value, ('role', 'shard'), shift_perm(phase, step))  40 us
    all_to_all x3, starting transfers between devices, exchange(): lax.all_to_all(value, ('role', 'shard'), 0, 0, axis_index_groups=plane_gr...  17.9 us
    all_to_all x3, waiting for transfers between devices, exchange(): lax.all_to_all(value, ('role', 'shard'), 0, 0, axis_index_groups=plane_gr...  15.3 us
    ppermute x10, starting transfers between devices, send(): return lax.ppermute(value, ('role', 'shard'), shift_perm(phase, step))  14.8 us
    pallas_call x2, Pallas kernels, make_products(): pl.pallas_call(functools.partial(products_kernel, count), out_shape=[jax....  13 us
    pallas_call x1, Pallas kernels, make_weights(): pl.pallas_call(weights_kernel, out_shape=[jax.ShapeDtypeStruct((depth, 2...  11.7 us
    ppermute x9, starting transfers between devices, swap(): return lax.ppermute(value, 'role', [(0, 1), (1, 0)])  11 us
    pallas_call x1, Pallas kernels, make_down(): pl.pallas_call(down_kernel, out_shape=[jax.ShapeDtypeStruct((rows // 4, c...  4.88 us
  transfers between devices with their start and end apart: 22, of which 10 were waited for; matrix products, arithmetic and copies ran while one was open for 7% of the time, Pallas kernels for 20%

profile of v3, /device:TPU:1, one launch (start us, length us, event | category | flops | bytes accessed | tf_op | source)
XLA Modules:
  0.0 158.7 jit_solution(16488240550577236620)
XLA Ops:
  1.1 1.5 collective-permute-start
  4.3 3.6 %fusion.92 = (f32[8,2,16]{2,1,0:T(2,128)S(1)}, f32[8,2,16,1024]{3,2,1,0:T(8,128)S(1)}) fusion(bf16[8,2,16,128]{3,0,2,1:T(8,128)(2,1)} %bitcast.66, pred[8,1024]{1,0:T(8,128)(4,1)S(1)} %iota_compare_fusion.3, bf16[8,1024,256]{2,1,0:T(8,128)(2,1)} %param.21), kind=kOutput, calls=%fused_computation.247 | convolution fusion | flops 67895040 | bytes 5317632 | tf_op jit(solution)/shard_map/skgd,slkd->skgl/dot_general | solution.py:35
  9.5 3.1 %collective-permute-start.1 = (bf16[64,4096]{1,0:T(8,128)(2,1)S(1)}, bf16[64,4096]{1,0:T(8,128)(2,1)S(1)}, u32[]{:S(2)}, u32[]{:S(2)}) collective-permute-start(bf16[64,4096]{1,0:T(8,128)(2,1)S(1)} %get-tuple-element.50), channel_id=1, source_target_pairs={{0,32},{1,33},{2,34},{3,35},{4,36},{5,37},{6,38},{7,39},{8,40},{9,... | collective-permute-start | bytes 1572872 | tf_op jit(solution)/shard_map/ppermute | solution.py:132
  13.6 7.6 %all-to-all-start = ((bf16[16,8,4096]{2,1,0:T(8,128)(2,1)}), bf16[16,8,4096]{2,1,0:T(8,128)(2,1)S(1)}, u32[]{:S(2)}, u32[]{:S(2)}) async-start(bf16[16,8,4096]{2,1,0:T(8,128)(2,1)} %broadcast_in_dim.46), calls=%async_computation | async-start | bytes 2097152 | tf_op jit(solution)/shard_map/all_to_all | solution.py:155
  21.3 11.7 %shard_map.172 = (bf16[8192,512]{1,0:T(8,128)(2,1)}, bf16[256,4096]{1,0:T(8,128)(2,1)S(1)}, bf16[256,4096]{1,0:T(8,128)(2,1)}, bf16[16,128]{1,0:T(8,128)(2,1)S(1)}) custom-call(s32[1]{0:T(128)} %bitcast.7.role, bf16[8192,256]{1,0:T(8,128)(2,1)} %gate_ref.1, f32[64,256]{1,0:T(8,128)S(1)} %copy-done.9, bf16[8192,256]{1,0:T(8,128)(2,1)} %up_ref.1, ...), custom_call_target="tpu_custom_call" | custom-call | flops 25165824 | bytes 25165824 | tf_op jit(solution)/shard_map/pallas_call | solution.py:89
  40.4 2.0 %collective-permute-start.14 = (bf16[256,4096]{1,0:T(8,128)(2,1)}, bf16[256,4096]{1,0:T(8,128)(2,1)}, u32[]{:S(2)}, u32[]{:S(2)}) collective-permute-start(bf16[256,4096]{1,0:T(8,128)(2,1)} %get-tuple-element.40), channel_id=1, source_target_pairs={{0,64},{64,0},{1,65},{65,1},{2,66},{66,2},{3,67},{67,3},{4,68},{68... | collective-permute-start | bytes 6291464 | tf_op jit(solution)/shard_map/ppermute | solution.py:136
  43.3 9.6 %collective-permute-done.2.x1.refs_1_ = bf16[128,4096]{1,0:T(8,128)(2,1)S(1)} collective-permute-done((bf16[128,4096]{1,0:T(8,128)(2,1)S(1)}, bf16[128,4096]{1,0:T(8,128)(2,1)S(1)}, u32[]{:S(2)}, u32[]{:S(2)}) %collective-permute-start.2) | collective-permute-done | bytes 1048608 | tf_op jit(solution)/shard_map/ppermute | solution.py:132
  52.9 2.2 %collective-permute-start.5 = (bf16[128,4096]{1,0:T(8,128)(2,1)S(1)}, bf16[128,4096]{1,0:T(8,128)(2,1)}, u32[]{:S(2)}, u32[]{:S(2)}) collective-permute-start(bf16[128,4096]{1,0:T(8,128)(2,1)S(1)} %collective-permute-done.2.x1.refs_1_), channel_id=1, source_target_pairs={{0,64},{64,0},{1,65},{65,1},{2,66},{66,2},{3,67},{67,3},{4,68},{68... | collective-permute-start | bytes 3145736 | tf_op jit(solution)/shard_map/ppermute | solution.py:136
  55.9 3.5 %shard_map.173 = f32[16,16,384]{2,1,0:T(8,128)} custom-call(s32[8]{0:T(128)S(1)} %pad_add_fusion.3.ids, bf16[128,4096]{1,0:T(8,128)(2,1)S(1)} %fusion.19.x0.refs_0_, bf16[128,4096]{1,0:T(8,128)(2,1)S(1)} %collective-permute-done.2.x1.refs_1_, bf16[128,4096]{1,0:T(8,128)(2,1)} %collective-permute-done.3.x3.refs_2_, ...), custom_call_target="tpu_custom_call" | custom-call | flops 268435456 | bytes 5242880 | tf_op jit(solution)/shard_map/pallas_call | solution.py:199
  59.5 4.9 %all-to-all-start.1 = ((f32[16,16,384]{2,1,0:T(8,128)}), f32[16,16,384]{2,1,0:T(8,128)}, u32[]{:S(2)}, u32[]{:S(2)}) async-start(f32[16,16,384]{2,1,0:T(8,128)} %shard_map.173), calls=%async_computation.1 | async-start | bytes 786432 | tf_op jit(solution)/shard_map/all_to_all | solution.py:155
  66.4 7.7 %shard_map.174 = (f32[384,512]{1,0:T(8,128)S(1)}, f32[384,512]{1,0:T(8,128)S(1)}, f32[384,128]{1,0:T(8,128)S(1)}, f32[384,128]{1,0:T(8,128)S(1)}, f32[8,4096]{1,0:T(8,128)S(1)}) custom-call(bf16[128,4096]{1,0:T(8,128)(2,1)S(1)} %fusion.19.x0.refs_0_, bf16[128,4096]{1,0:T(8,128)(2,1)S(1)} %collective-permute-done.2.x1.refs_1_, ...), custom_call_target="tpu_custom_call" | custom-call | flops 3221225472 | bytes 18874368 | tf_op jit(solution)/shard_map/pallas_call | solution.py:239
  77.6 4.1 %collective-permute-done.7.refs_0_ = bf16[128,4096]{1,0:T(8,128)(2,1)S(1)} collective-permute-done((bf16[128,4096]{1,0:T(8,128)(2,1)S(1)}, bf16[128,4096]{1,0:T(8,128)(2,1)S(1)}, u32[]{:S(2)}, u32[]{:S(2)}) %collective-permute-start.7) | collective-permute-done | bytes 1048608 | tf_op jit(solution)/shard_map/ppermute | solution.py:132
  82.3 2.5 %collective-permute-start.10 = (f32[16,384]{1,0:T(8,128)S(1)}, f32[16,384]{1,0:T(8,128)S(1)}, u32[]{:S(2)}, u32[]{:S(2)}) collective-permute-start(f32[16,384]{1,0:T(8,128)S(1)} %add_reduce_fusion), channel_id=1, source_target_pairs={{0,48},{1,49},{2,50},{3,51},{4,52},{5,53},{6,54},{7,55},{8,56},{9,... | collective-permute-start | bytes 73736 | tf_op jit(solution)/shard_map/ppermute | solution.py:132
  86.0 2.9 %collective-permute-done.11 = f32[16,384]{1,0:T(8,128)S(1)} collective-permute-done((f32[16,384]{1,0:T(8,128)S(1)}, f32[16,384]{1,0:T(8,128)S(1)}, u32[]{:S(2)}, u32[]{:S(2)}) %collective-permute-start.11) | collective-permute-done | bytes 24608 | tf_op jit(solution)/shard_map/ppermute | solution.py:132
  90.6 5.3 %shard_map.175 = (f32[128,512]{1,0:T(8,128)S(1)}, f32[128,512]{1,0:T(8,128)S(1)}, f32[128,128]{1,0:T(8,128)S(1)}, f32[128,128]{1,0:T(8,128)S(1)}, f32[8,4096]{1,0:T(8,128)S(1)}) custom-call(bf16[128,4096]{1,0:T(8,128)(2,1)S(1)} %collective-permute-done.7.refs_0_, bf16[128,4096]{1,0:T(8,128)(2,1)S(1)} %collective-permute-done.8.refs_1_, ...), custom_call_target="tpu_custom_call" | custom-call | flops 1073741824 | bytes 14680064 | tf_op jit(solution)/shard_map/pallas_call | solution.py:239
  96.3 3.1 %shard_map.176 = (bf16[512,256]{1,0:T(8,128)(2,1)S(1)}, bf16[512,256]{1,0:T(8,128)(2,1)S(1)}) custom-call(s32[2]{0:T(128)S(1)} %pad_add_fusion.4.place, f32[384,512]{1,0:T(8,128)S(1)} %copy-done.4, f32[384,512]{1,0:T(8,128)S(1)} %copy-done.6, f32[384,128]{1,0:T(8,128)S(1)} %get-tuple-element.31.own_sq_a, f32[384,128]{1,0:T(8,128)S(1)} %get-tuple-element.32.other_sq_a, ...), custom_call_target="tpu_custom_call" | custom-call | flops 1073741824 | bytes 6291456 | tf_op jit(solution)/shard_map/pallas_call | solution.py:318
  101.1 4.9 %shard_map.177 = (f32[128,4096]{1,0:T(8,128)S(1)}, bf16[128,4096]{1,0:T(8,128)(2,1)S(1)}, bf16[128,4096]{1,0:T(8,128)(2,1)S(1)}, bf16[128,4096]{1,0:T(8,128)(2,1)S(1)}) custom-call(bf16[512,256]{1,0:T(8,128)(2,1)S(1)} %get-tuple-element.37.mine_ref, bf16[512,256]{1,0:T(8,128)(2,1)S(1)} %collective-permute-done.13.other_ref, bf16[256,4096]{1,0:T(8,128)(2,1)} %copy-done.12, ...), custom_call_target="tpu_custom_call" | custom-call | flops 2147483648 | bytes 9437184 | tf_op jit(solution)/shard_map/pallas_call | solution.py:345
  107.9 2.2 %collective-permute-start.17 = (bf16[128,4096]{1,0:T(8,128)(2,1)S(1)}, bf16[128,4096]{1,0:T(8,128)(2,1)S(1)}, u32[]{:S(2)}, u32[]{:S(2)}) collective-permute-start(bf16[128,4096]{1,0:T(8,128)(2,1)S(1)} %get-tuple-element.44), channel_id=1, source_target_pairs={{0,48},{1,49},{2,50},{3,51},{4,52},{5,53},{6,54},{7,55},{8,56},{9,... | collective-permute-start | bytes 3145736 | tf_op jit(solution)/shard_map/ppermute | solution.py:132
  110.1 11.5 %collective-permute-done.15 = bf16[128,4096]{1,0:T(8,128)(2,1)S(1)} collective-permute-done((bf16[128,4096]{1,0:T(8,128)(2,1)S(1)}, bf16[128,4096]{1,0:T(8,128)(2,1)S(1)}, u32[]{:S(2)}, u32[]{:S(2)}) %collective-permute-start.15) | collective-permute-done | bytes 1048608 | tf_op jit(solution)/shard_map/ppermute | solution.py:132
  121.5 11.2 %collective-permute-done.16 = bf16[128,4096]{1,0:T(8,128)(2,1)S(1)} collective-permute-done((bf16[128,4096]{1,0:T(8,128)(2,1)S(1)}, bf16[128,4096]{1,0:T(8,128)(2,1)S(1)}, u32[]{:S(2)}, u32[]{:S(2)}) %collective-permute-start.16) | collective-permute-done | bytes 1048608 | tf_op jit(solution)/shard_map/ppermute | solution.py:132
  132.7 1.5 fusion.18
  134.3 5.4 %all-to-all-start.2 = ((bf16[16,8,4096]{2,1,0:T(8,128)(2,1)}), bf16[16,8,4096]{2,1,0:T(8,128)(2,1)S(1)}, u32[]{:S(2)}, u32[]{:S(2)}) async-start(bf16[16,8,4096]{2,1,0:T(8,128)(2,1)} %fusion.18), calls=%async_computation.2 | async-start | bytes 2097152 | tf_op jit(solution)/shard_map/all_to_all | solution.py:155
  139.7 14.0 %all-to-all-done.2 = bf16[16,8,4096]{2,1,0:T(8,128)(2,1)S(1)} async-done(((bf16[16,8,4096]{2,1,0:T(8,128)(2,1)}), bf16[16,8,4096]{2,1,0:T(8,128)(2,1)S(1)}, u32[]{:S(2)}, u32[]{:S(2)}) %all-to-all-start.2) | async-done | bytes 1048608 | tf_op jit(solution)/shard_map/all_to_all | solution.py:155
  153.9 3.2 %collective-permute-start.18 = (bf16[4,4096]{1,0:T(4,128)(2,1)S(1)}, bf16[4,4096]{1,0:T(4,128)(2,1)S(1)}, u32[]{:S(2)}, u32[]{:S(2)}) collective-permute-start(bf16[4,4096]{1,0:T(4,128)(2,1)S(1)} %constant_dynamic-slice_fusion), channel_id=1, source_target_pairs={{0,64},{64,0},{1,65},{65,1},{2,66},{66,2},{3,67},{67,3},{4,68},{68... | collective-permute-start | bytes 98312 | tf_op jit(solution)/shard_map/ppermute | solution.py:136
  (117 shorter events, 28.8 us)
Async XLA Ops:
  1.1 8.2 %collective-permute-start = (bf16[32,4096]{1,0:T(8,128)(2,1)S(1)}, bf16[32,4096]{1,0:T(8,128)(2,1)S(1)}, u32[]{:S(2)}, u32[]{:S(2)}) collective-permute-start(bf16[32,4096]{1,0:T(8,128)(2,1)S(1)} %get-tuple-element.52), channel_id=1, source_target_pairs={{0,64},{64,0},{1,65},{65,1},{2,66},{66,2},{3,67},{67,3},{4,68},{68... | collective-permute-start | bytes 786440 | tf_op jit(solution)/shard_map/ppermute | solution.py:136
  9.5 24.9 %collective-permute-start.1 = (bf16[64,4096]{1,0:T(8,128)(2,1)S(1)}, bf16[64,4096]{1,0:T(8,128)(2,1)S(1)}, u32[]{:S(2)}, u32[]{:S(2)}) collective-permute-start(bf16[64,4096]{1,0:T(8,128)(2,1)S(1)} %get-tuple-element.50), channel_id=1, source_target_pairs={{0,32},{1,33},{2,34},{3,35},{4,36},{5,37},{6,38},{7,39},{8,40},{9,... | collective-permute-start | bytes 1572872 | tf_op jit(solution)/shard_map/ppermute | solution.py:132
  13.6 22.9 %all-to-all-start = ((bf16[16,8,4096]{2,1,0:T(8,128)(2,1)}), bf16[16,8,4096]{2,1,0:T(8,128)(2,1)S(1)}, u32[]{:S(2)}, u32[]{:S(2)}) async-start(bf16[16,8,4096]{2,1,0:T(8,128)(2,1)} %broadcast_in_dim.46), calls=%async_computation | async-start | bytes 2097152 | tf_op jit(solution)/shard_map/all_to_all | solution.py:155
  37.7 15.2 %collective-permute-start.2 = (bf16[128,4096]{1,0:T(8,128)(2,1)S(1)}, bf16[128,4096]{1,0:T(8,128)(2,1)S(1)}, u32[]{:S(2)}, u32[]{:S(2)}) collective-permute-start(bf16[128,4096]{1,0:T(8,128)(2,1)S(1)} %fusion.19.x0.refs_0_), channel_id=1, source_target_pairs={{0,16},{1,17},{2,18},{3,19},{4,20},{5,21},{6,22},{7,23},{8,24},{9,... | collective-permute-start | bytes 3145736 | tf_op jit(solution)/shard_map/ppermute | solution.py:132
  39.0 16.1 %collective-permute-start.3 = (bf16[128,4096]{1,0:T(8,128)(2,1)S(1)}, bf16[128,4096]{1,0:T(8,128)(2,1)}, u32[]{:S(2)}, u32[]{:S(2)}) collective-permute-start(bf16[128,4096]{1,0:T(8,128)(2,1)S(1)} %fusion.19.x0.refs_0_), channel_id=1, source_target_pairs={{0,48},{1,49},{2,50},{3,51},{4,52},{5,53},{6,54},{7,55},{8,56},{9,... | collective-permute-start | bytes 3145736 | tf_op jit(solution)/shard_map/ppermute | solution.py:132
  40.4 59.2 %collective-permute-start.14 = (bf16[256,4096]{1,0:T(8,128)(2,1)}, bf16[256,4096]{1,0:T(8,128)(2,1)}, u32[]{:S(2)}, u32[]{:S(2)}) collective-permute-start(bf16[256,4096]{1,0:T(8,128)(2,1)} %get-tuple-element.40), channel_id=1, source_target_pairs={{0,64},{64,0},{1,65},{65,1},{2,66},{66,2},{3,67},{67,3},{4,68},{68... | collective-permute-start | bytes 6291464 | tf_op jit(solution)/shard_map/ppermute | solution.py:136
  43.2 23.2 %collective-permute-start.4 = (bf16[128,4096]{1,0:T(8,128)(2,1)S(1)}, bf16[128,4096]{1,0:T(8,128)(2,1)}, u32[]{:S(2)}, u32[]{:S(2)}) collective-permute-start(bf16[128,4096]{1,0:T(8,128)(2,1)S(1)} %fusion.19.x0.refs_0_), channel_id=1, source_target_pairs={{0,64},{64,0},{1,65},{65,1},{2,66},{66,2},{3,67},{67,3},{4,68},{68... | collective-permute-start | bytes 3145736 | tf_op jit(solution)/shard_map/ppermute | solution.py:136
  52.9 13.5 %collective-permute-start.5 = (bf16[128,4096]{1,0:T(8,128)(2,1)S(1)}, bf16[128,4096]{1,0:T(8,128)(2,1)}, u32[]{:S(2)}, u32[]{:S(2)}) collective-permute-start(bf16[128,4096]{1,0:T(8,128)(2,1)S(1)} %collective-permute-done.2.x1.refs_1_), channel_id=1, source_target_pairs={{0,64},{64,0},{1,65},{65,1},{2,66},{66,2},{3,67},{67,3},{4,68},{68... | collective-permute-start | bytes 3145736 | tf_op jit(solution)/shard_map/ppermute | solution.py:136
  55.2 11.2 %collective-permute-start.6 = (bf16[128,4096]{1,0:T(8,128)(2,1)}, bf16[128,4096]{1,0:T(8,128)(2,1)}, u32[]{:S(2)}, u32[]{:S(2)}) collective-permute-start(bf16[128,4096]{1,0:T(8,128)(2,1)} %collective-permute-done.3.x3.refs_2_), channel_id=1, source_target_pairs={{0,64},{64,0},{1,65},{65,1},{2,66},{66,2},{3,67},{67,3},{4,68},{68... | collective-permute-start | bytes 3145736 | tf_op jit(solution)/shard_map/ppermute | solution.py:136
  59.5 17.0 %all-to-all-start.1 = ((f32[16,16,384]{2,1,0:T(8,128)}), f32[16,16,384]{2,1,0:T(8,128)}, u32[]{:S(2)}, u32[]{:S(2)}) async-start(f32[16,16,384]{2,1,0:T(8,128)} %shard_map.173), calls=%async_computation.1 | async-start | bytes 786432 | tf_op jit(solution)/shard_map/all_to_all | solution.py:155
  64.4 17.3 %collective-permute-start.7 = (bf16[128,4096]{1,0:T(8,128)(2,1)S(1)}, bf16[128,4096]{1,0:T(8,128)(2,1)S(1)}, u32[]{:S(2)}, u32[]{:S(2)}) collective-permute-start(bf16[128,4096]{1,0:T(8,128)(2,1)S(1)} %collective-permute-done.2.x1.refs_1_), channel_id=1, source_target_pairs={{0,16},{1,17},{2,18},{3,19},{4,20},{5,21},{6,22},{7,23},{8,24},{9,... | collective-permute-start | bytes 3145736 | tf_op jit(solution)/shard_map/ppermute | solution.py:132
  81.8 8.8 %collective-permute-start.8 = (bf16[128,4096]{1,0:T(8,128)(2,1)S(1)}, bf16[128,4096]{1,0:T(8,128)(2,1)S(1)}, u32[]{:S(2)}, u32[]{:S(2)}) collective-permute-start(bf16[128,4096]{1,0:T(8,128)(2,1)S(1)} %pad_add_fusion), channel_id=1, source_target_pairs={{0,64},{64,0},{1,65},{65,1},{2,66},{66,2},{3,67},{67,3},{4,68},{68... | collective-permute-start | bytes 3145736 | tf_op jit(solution)/shard_map/ppermute | solution.py:136
  82.3 3.7 %collective-permute-start.10 = (f32[16,384]{1,0:T(8,128)S(1)}, f32[16,384]{1,0:T(8,128)S(1)}, u32[]{:S(2)}, u32[]{:S(2)}) collective-permute-start(f32[16,384]{1,0:T(8,128)S(1)} %add_reduce_fusion), channel_id=1, source_target_pairs={{0,48},{1,49},{2,50},{3,51},{4,52},{5,53},{6,54},{7,55},{8,56},{9,... | collective-permute-start | bytes 73736 | tf_op jit(solution)/shard_map/ppermute | solution.py:132
  84.8 4.2 %collective-permute-start.11 = (f32[16,384]{1,0:T(8,128)S(1)}, f32[16,384]{1,0:T(8,128)S(1)}, u32[]{:S(2)}, u32[]{:S(2)}) collective-permute-start(f32[16,384]{1,0:T(8,128)S(1)} %add_reduce_fusion), channel_id=1, source_target_pairs={{0,32},{1,33},{2,34},{3,35},{4,36},{5,37},{6,38},{7,39},{8,40},{9,... | collective-permute-start | bytes 73736 | tf_op jit(solution)/shard_map/ppermute | solution.py:132
  85.4 4.2 %collective-permute-start.9 = (f32[16,384]{1,0:T(8,128)S(1)}, f32[16,384]{1,0:T(8,128)S(1)}, u32[]{:S(2)}, u32[]{:S(2)}) collective-permute-start(f32[16,384]{1,0:T(8,128)S(1)} %add_reduce_fusion), channel_id=1, source_target_pairs={{0,16},{1,17},{2,18},{3,19},{4,20},{5,21},{6,22},{7,23},{8,24},{9,... | collective-permute-start | bytes 73736 | tf_op jit(solution)/shard_map/ppermute | solution.py:132
  89.6 6.3 %collective-permute-start.12 = (f32[16,512]{1,0:T(8,128)S(1)}, f32[16,512]{1,0:T(8,128)S(1)}, u32[]{:S(2)}, u32[]{:S(2)}) collective-permute-start(f32[16,512]{1,0:T(8,128)S(1)} %pad_maximum_fusion.2.low_ref), channel_id=1, source_target_pairs={{0,64},{64,0},{1,65},{65,1},{2,66},{66,2},{3,67},{67,3},{4,68},{68... | collective-permute-start | bytes 98312 | tf_op jit(solution)/shard_map/ppermute | solution.py:136
  99.5 1.6 %collective-permute-start.13 = (bf16[512,256]{1,0:T(8,128)(2,1)S(1)}, bf16[512,256]{1,0:T(8,128)(2,1)S(1)}, u32[]{:S(2)}, u32[]{:S(2)}) collective-permute-start(bf16[512,256]{1,0:T(8,128)(2,1)S(1)} %get-tuple-element.38), channel_id=1, source_target_pairs={{0,64},{64,0},{1,65},{65,1},{2,66},{66,2},{3,67},{67,3},{4,68},{68... | collective-permute-start | bytes 786440 | tf_op jit(solution)/shard_map/ppermute | solution.py:136
  106.0 15.6 %collective-permute-start.15 = (bf16[128,4096]{1,0:T(8,128)(2,1)S(1)}, bf16[128,4096]{1,0:T(8,128)(2,1)S(1)}, u32[]{:S(2)}, u32[]{:S(2)}) collective-permute-start(bf16[128,4096]{1,0:T(8,128)(2,1)S(1)} %get-tuple-element.42), channel_id=1, source_target_pairs={{0,32},{1,33},{2,34},{3,35},{4,36},{5,37},{6,38},{7,39},{8,40},{9,... | collective-permute-start | bytes 3145736 | tf_op jit(solution)/shard_map/ppermute | solution.py:132
  107.4 25.3 %collective-permute-start.16 = (bf16[128,4096]{1,0:T(8,128)(2,1)S(1)}, bf16[128,4096]{1,0:T(8,128)(2,1)S(1)}, u32[]{:S(2)}, u32[]{:S(2)}) collective-permute-start(bf16[128,4096]{1,0:T(8,128)(2,1)S(1)} %get-tuple-element.43), channel_id=1, source_target_pairs={{0,16},{1,17},{2,18},{3,19},{4,20},{5,21},{6,22},{7,23},{8,24},{9,... | collective-permute-start | bytes 3145736 | tf_op jit(solution)/shard_map/ppermute | solution.py:132
  107.9 24.8 %collective-permute-start.17 = (bf16[128,4096]{1,0:T(8,128)(2,1)S(1)}, bf16[128,4096]{1,0:T(8,128)(2,1)S(1)}, u32[]{:S(2)}, u32[]{:S(2)}) collective-permute-start(bf16[128,4096]{1,0:T(8,128)(2,1)S(1)} %get-tuple-element.44), channel_id=1, source_target_pairs={{0,48},{1,49},{2,50},{3,51},{4,52},{5,53},{6,54},{7,55},{8,56},{9,... | collective-permute-start | bytes 3145736 | tf_op jit(solution)/shard_map/ppermute | solution.py:132
  132.7 26.0 %copy-start.1 = (bf16[8,256]{1,0:T(8,128)(2,1)S(1)}, bf16[8,256]{1,0:T(8,128)(2,1)}, u32[]{:S(2)}) copy-start(bf16[8,256]{1,0:T(8,128)(2,1)} %param.19) | copy-start | bytes 12292
  134.3 19.5 %copy-start.8 = (f32[8,4096]{1,0:T(8,128)S(1)}, f32[8,4096]{1,0:T(8,128)}, u32[]{:S(2)}) copy-start(f32[8,4096]{1,0:T(8,128)} %copy-done.7) | copy-start | bytes 393220
  134.3 19.4 %all-to-all-start.2 = ((bf16[16,8,4096]{2,1,0:T(8,128)(2,1)}), bf16[16,8,4096]{2,1,0:T(8,128)(2,1)S(1)}, u32[]{:S(2)}, u32[]{:S(2)}) async-start(bf16[16,8,4096]{2,1,0:T(8,128)(2,1)} %fusion.18), calls=%async_computation.2 | async-start | bytes 2097152 | tf_op jit(solution)/shard_map/all_to_all | solution.py:155
  153.9 4.1 %collective-permute-start.18 = (bf16[4,4096]{1,0:T(4,128)(2,1)S(1)}, bf16[4,4096]{1,0:T(4,128)(2,1)S(1)}, u32[]{:S(2)}, u32[]{:S(2)}) collective-permute-start(bf16[4,4096]{1,0:T(4,128)(2,1)S(1)} %constant_dynamic-slice_fusion), channel_id=1, source_target_pairs={{0,64},{64,0},{1,65},{65,1},{2,66},{66,2},{3,67},{67,3},{4,68},{68... | collective-permute-start | bytes 98312 | tf_op jit(solution)/shard_map/ppermute | solution.py:136
  (17 other events, 97.0 us)

commit v4 on v3

--- a/solution.py
+++ b/solution.py
@@ -328,26 +328,36 @@
     )(place, *first, *second, low, low_other, ids, pos_mine, pos_other, maps)
 
 
-def down_kernel(mine_ref, other_ref, keep_ref, recv_ref, o0, o1, o2, o3):
+def down_kernel(mine_ref, other_ref, keep_ref, recv_ref, *outs):
     rows = jnp.concatenate([mine_ref[...], other_ref[...]], axis=1)
     weights = jnp.concatenate([keep_ref[...], recv_ref[...]], axis=0)
     total = jnp.dot(rows, weights, preferred_element_type=F32)
-    for step, out in enumerate((o0, o1, o2, o3)):
-        out[...] = total[step * 128 : (step + 1) * 128].astype(out.dtype)
+    i = pl.program_id(0)
+    half = pl.num_programs(0) // 2
+    for group, here in ((outs[:4], i < half), (outs[4:], i >= half)):
+
+        @pl.when(here)
+        def _():
+            for step, out in enumerate(group):
+                out[...] = total[step * 128 : (step + 1) * 128].astype(out.dtype)
 
 
 def make_down(mine, other, keep, recv):
     rows, width = mine.shape
     columns = keep.shape[1]
     step = 1024
+    half = columns // step // 2
     whole = lambda x: pl.BlockSpec(x.shape, lambda i: (0, 0))
-    tile = lambda n: pl.BlockSpec((n, step), lambda i: (0, i))
+    tile = pl.BlockSpec((width, step), lambda i: (0, i))
+    left = pl.BlockSpec((rows // 4, step), lambda i: (0, jnp.minimum(i, half - 1)))
+    right = pl.BlockSpec((rows // 4, step), lambda i: (0, jnp.maximum(i - half, 0)))
+    kinds = [F32, BF, BF, BF] * 2
     return pl.pallas_call(
         down_kernel,
-        out_shape=[jax.ShapeDtypeStruct((rows // 4, columns), F32 if d == 0 else BF) for d in range(4)],
+        out_shape=[jax.ShapeDtypeStruct((rows // 4, columns // 2), kind) for kind in kinds],
         grid=(columns // step,),
-        in_specs=[whole(mine), whole(other), tile(width), tile(width)],
-        out_specs=[tile(rows // 4)] * 4,
+        in_specs=[whole(mine), whole(other), tile, tile],
+        out_specs=[left] * 4 + [right] * 4,
         compiler_params=pltpu.CompilerParams(vmem_limit_bytes=48 * 1024 * 1024),
         cost_estimate=pl.CostEstimate(
             flops=4 * rows * width * columns, bytes_accessed=9 * 1024 * 1024, transcendentals=0
@@ -488,10 +498,13 @@
     hidden_other = swap(hidden_send)
 
     pieces = make_down(hidden, hidden_other, down_keep, down_recv)
-    got = [send(pieces[step], 2, step) for step in (2, 1, 3)]
-    total = pieces[0] + got[0].astype(F32) + got[1].astype(F32) + got[2].astype(F32)
-    part = total.astype(BF).reshape(16, 8, half)
-    total = jnp.sum(exchange(part).astype(F32), axis=0)
+    totals = []
+    for side in (pieces[:4], pieces[4:]):
+        got = [send(side[step], 2, step) for step in (2, 1, 3)]
+        total = side[0] + got[0].astype(F32) + got[1].astype(F32) + got[2].astype(F32)
+        total = exchange(total.astype(BF).reshape(16, 8, half // 2))
+        totals.append(jnp.sum(total.astype(F32), axis=0))
+    total = jnp.concatenate(totals, axis=1)
     result = (base + base_far + total).astype(BF)
     keep = lax.dynamic_slice(result, (role * 4, 0), (4, half))
     got = swap(lax.dynamic_slice(result, ((1 - role) * 4, 0), (4, half)))

time: 160 us -> 159 us (level)
  waiting for transfers between devices: 57.6 us -> 46.1 us
  starting transfers between devices: 43.7 us -> 49.7 us
  other arithmetic: 8.63 us -> 11.8 us
    ppermute x10 -> x13, waiting for transfers between devices: 40 us -> 31.8 us  [send(): return lax.ppermute(value, ('role', 'shard'), shift_perm(phase, step))]
    all_to_all x3 -> x4, starting transfers between devices: 17.9 us -> 22.8 us  [exchange(): lax.all_to_all(value, ('role', 'shard'), 0, 0, axis_index_groups=plane_gr...]
    all_to_all x3 -> x4, waiting for transfers between devices: 15.3 us -> 11.9 us  [exchange(): lax.all_to_all(value, ('role', 'shard'), 0, 0, axis_index_groups=plane_gr...]
    reshape x1 -> x2, other arithmetic: 1.54 us -> 3.58 us  [local(): total = exchange(total.astype(BF).reshape(16, 8, half // 2))]
    ppermute x10 -> x13, starting transfers between devices: 14.8 us -> 16.7 us  [send(): return lax.ppermute(value, ('role', 'shard'), shift_perm(phase, step))]
    unnamed x38 -> x40, local copies, waits for them, and re-layouts: 3.94 us -> 5.22 us
  transfers between devices with their start and end apart: 22 -> 26, of which waited for: 10 -> 12; matrix products, arithmetic and copies ran while one was open for 7% -> 10% of each run, Pallas kernels for 20% -> 20%
where the time goes in v4:
time: 159 us; the launch traced here: 158 us
  starting transfers between devices  49.7 us (31%)
  waiting for transfers between devices  46.1 us (29%)
  Pallas kernels  36.2 us (23%)
  other arithmetic  11.8 us (7%)
  local copies, waits for them, and re-layouts  7.95 us (5%)
  matrix products  5.28 us (3%)
    ppermute x13, waiting for transfers between devices, send(): return lax.ppermute(value, ('role', 'shard'), shift_perm(phase, step))  31.8 us
    all_to_all x4, starting transfers between devices, exchange(): lax.all_to_all(value, ('role', 'shard'), 0, 0, axis_index_groups=plane_gr...  22.8 us
    ppermute x13, starting transfers between devices, send(): return lax.ppermute(value, ('role', 'shard'), shift_perm(phase, step))  16.7 us
    pallas_call x2, Pallas kernels, make_products(): pl.pallas_call(functools.partial(products_kernel, count), out_shape=[jax....  13 us
    all_to_all x4, waiting for transfers between devices, exchange(): lax.all_to_all(value, ('role', 'shard'), 0, 0, axis_index_groups=plane_gr...  11.9 us
    pallas_call x1, Pallas kernels, make_weights(): pl.pallas_call(weights_kernel, out_shape=[jax.ShapeDtypeStruct((depth, 2...  11.2 us
    ppermute x9, starting transfers between devices, swap(): return lax.ppermute(value, 'role', [(0, 1), (1, 0)])  10.3 us
    pallas_call x1, Pallas kernels, make_down(): pl.pallas_call(down_kernel, out_shape=[jax.ShapeDtypeStruct((rows // 4, c...  5.34 us
  transfers between devices with their start and end apart: 26, of which 12 were waited for; matrix products, arithmetic and copies ran while one was open for 10% of the time, Pallas kernels for 20%

profile of v4, /device:TPU:1, one launch (start us, length us, event | category | flops | bytes accessed | tf_op | source)
XLA Modules:
  0.0 157.7 jit_solution(2043297237410279167)
XLA Ops:
  4.4 3.5 %fusion.94 = (f32[8,2,16]{2,1,0:T(2,128)S(1)}, f32[8,2,16,1024]{3,2,1,0:T(8,128)S(1)}) fusion(bf16[8,2,16,128]{3,0,2,1:T(8,128)(2,1)} %bitcast.68, pred[8,1024]{1,0:T(8,128)(4,1)S(1)} %iota_compare_fusion.3, bf16[8,1024,256]{2,1,0:T(8,128)(2,1)} %param.21), kind=kOutput, calls=%fused_computation.251 | convolution fusion | flops 67895040 | bytes 5317632 | tf_op jit(solution)/shard_map/skgd,slkd->skgl/dot_general | solution.py:35
  9.4 3.1 %collective-permute-start.1 = (bf16[64,4096]{1,0:T(8,128)(2,1)S(1)}, bf16[64,4096]{1,0:T(8,128)(2,1)S(1)}, u32[]{:S(2)}, u32[]{:S(2)}) collective-permute-start(bf16[64,4096]{1,0:T(8,128)(2,1)S(1)} %get-tuple-element.58), channel_id=1, source_target_pairs={{0,32},{1,33},{2,34},{3,35},{4,36},{5,37},{6,38},{7,39},{8,40},{9,... | collective-permute-start | bytes 1572872 | tf_op jit(solution)/shard_map/ppermute | solution.py:132
  13.6 7.6 %all-to-all-start = ((bf16[16,8,4096]{2,1,0:T(8,128)(2,1)}), bf16[16,8,4096]{2,1,0:T(8,128)(2,1)S(1)}, u32[]{:S(2)}, u32[]{:S(2)}) async-start(bf16[16,8,4096]{2,1,0:T(8,128)(2,1)} %broadcast_in_dim.46), calls=%async_computation | async-start | bytes 2097152 | tf_op jit(solution)/shard_map/all_to_all | solution.py:155
  21.3 11.2 %shard_map.172 = (bf16[8192,512]{1,0:T(8,128)(2,1)}, bf16[256,4096]{1,0:T(8,128)(2,1)S(1)}, bf16[256,4096]{1,0:T(8,128)(2,1)S(1)}, bf16[16,128]{1,0:T(8,128)(2,1)S(1)}) custom-call(s32[1]{0:T(128)} %bitcast.7.role, bf16[8192,256]{1,0:T(8,128)(2,1)} %gate_ref.1, f32[64,256]{1,0:T(8,128)S(1)} %copy-done.9, bf16[8192,256]{1,0:T(8,128)(2,1)} %up_ref.1, ...), custom_call_target="tpu_custom_call" | custom-call | flops 25165824 | bytes 25165824 | tf_op jit(solution)/shard_map/pallas_call | solution.py:89
  43.2 9.6 %collective-permute-done.2.x1.refs_1_ = bf16[128,4096]{1,0:T(8,128)(2,1)S(1)} collective-permute-done((bf16[128,4096]{1,0:T(8,128)(2,1)S(1)}, bf16[128,4096]{1,0:T(8,128)(2,1)S(1)}, u32[]{:S(2)}, u32[]{:S(2)}) %collective-permute-start.2) | collective-permute-done | bytes 1048608 | tf_op jit(solution)/shard_map/ppermute | solution.py:132
  52.9 2.2 %collective-permute-start.5 = (bf16[128,4096]{1,0:T(8,128)(2,1)S(1)}, bf16[128,4096]{1,0:T(8,128)(2,1)}, u32[]{:S(2)}, u32[]{:S(2)}) collective-permute-start(bf16[128,4096]{1,0:T(8,128)(2,1)S(1)} %collective-permute-done.2.x1.refs_1_), channel_id=1, source_target_pairs={{0,64},{64,0},{1,65},{65,1},{2,66},{66,2},{3,67},{67,3},{4,68},{68... | collective-permute-start | bytes 3145736 | tf_op jit(solution)/shard_map/ppermute | solution.py:136
  55.9 3.5 %shard_map.173 = f32[16,16,384]{2,1,0:T(8,128)} custom-call(s32[8]{0:T(128)S(1)} %pad_add_fusion.3.ids, bf16[128,4096]{1,0:T(8,128)(2,1)S(1)} %fusion.18.x0.refs_0_, bf16[128,4096]{1,0:T(8,128)(2,1)S(1)} %collective-permute-done.2.x1.refs_1_, bf16[128,4096]{1,0:T(8,128)(2,1)} %collective-permute-done.3.x3.refs_2_, ...), custom_call_target="tpu_custom_call" | custom-call | flops 268435456 | bytes 5242880 | tf_op jit(solution)/shard_map/pallas_call | solution.py:199
  59.5 5.9 %all-to-all-start.1 = ((f32[16,16,384]{2,1,0:T(8,128)}), f32[16,16,384]{2,1,0:T(8,128)}, u32[]{:S(2)}, u32[]{:S(2)}) async-start(f32[16,16,384]{2,1,0:T(8,128)} %shard_map.173), calls=%async_computation.1 | async-start | bytes 786432 | tf_op jit(solution)/shard_map/all_to_all | solution.py:155
  67.4 7.7 %shard_map.174 = (f32[384,512]{1,0:T(8,128)S(1)}, f32[384,512]{1,0:T(8,128)S(1)}, f32[384,128]{1,0:T(8,128)S(1)}, f32[384,128]{1,0:T(8,128)S(1)}, f32[8,4096]{1,0:T(8,128)S(1)}) custom-call(bf16[128,4096]{1,0:T(8,128)(2,1)S(1)} %fusion.18.x0.refs_0_, bf16[128,4096]{1,0:T(8,128)(2,1)S(1)} %collective-permute-done.2.x1.refs_1_, ...), custom_call_target="tpu_custom_call" | custom-call | flops 3221225472 | bytes 18874368 | tf_op jit(solution)/shard_map/pallas_call | solution.py:239
  78.5 4.2 %collective-permute-done.7.refs_0_ = bf16[128,4096]{1,0:T(8,128)(2,1)S(1)} collective-permute-done((bf16[128,4096]{1,0:T(8,128)(2,1)S(1)}, bf16[128,4096]{1,0:T(8,128)(2,1)S(1)}, u32[]{:S(2)}, u32[]{:S(2)}) %collective-permute-start.7) | collective-permute-done | bytes 1048608 | tf_op jit(solution)/shard_map/ppermute | solution.py:132
  83.3 2.5 %collective-permute-start.10 = (f32[16,384]{1,0:T(8,128)S(1)}, f32[16,384]{1,0:T(8,128)S(1)}, u32[]{:S(2)}, u32[]{:S(2)}) collective-permute-start(f32[16,384]{1,0:T(8,128)S(1)} %add_reduce_fusion), channel_id=1, source_target_pairs={{0,48},{1,49},{2,50},{3,51},{4,52},{5,53},{6,54},{7,55},{8,56},{9,... | collective-permute-start | bytes 73736 | tf_op jit(solution)/shard_map/ppermute | solution.py:132
  87.0 2.9 %collective-permute-done.11 = f32[16,384]{1,0:T(8,128)S(1)} collective-permute-done((f32[16,384]{1,0:T(8,128)S(1)}, f32[16,384]{1,0:T(8,128)S(1)}, u32[]{:S(2)}, u32[]{:S(2)}) %collective-permute-start.11) | collective-permute-done | bytes 24608 | tf_op jit(solution)/shard_map/ppermute | solution.py:132
  91.6 5.3 %shard_map.175 = (f32[128,512]{1,0:T(8,128)S(1)}, f32[128,512]{1,0:T(8,128)S(1)}, f32[128,128]{1,0:T(8,128)S(1)}, f32[128,128]{1,0:T(8,128)S(1)}, f32[8,4096]{1,0:T(8,128)S(1)}) custom-call(bf16[128,4096]{1,0:T(8,128)(2,1)S(1)} %collective-permute-done.7.refs_0_, bf16[128,4096]{1,0:T(8,128)(2,1)S(1)} %collective-permute-done.8.refs_1_, ...), custom_call_target="tpu_custom_call" | custom-call | flops 1073741824 | bytes 14680064 | tf_op jit(solution)/shard_map/pallas_call | solution.py:239
  97.3 3.1 %shard_map.176 = (bf16[512,256]{1,0:T(8,128)(2,1)S(1)}, bf16[512,256]{1,0:T(8,128)(2,1)S(1)}) custom-call(s32[2]{0:T(128)S(1)} %pad_add_fusion.4.place, f32[384,512]{1,0:T(8,128)S(1)} %copy-done.4, f32[384,512]{1,0:T(8,128)S(1)} %copy-done.6, f32[384,128]{1,0:T(8,128)S(1)} %get-tuple-element.35.own_sq_a, f32[384,128]{1,0:T(8,128)S(1)} %get-tuple-element.36.other_sq_a, ...), custom_call_target="tpu_custom_call" | custom-call | flops 1073741824 | bytes 6291456 | tf_op jit(solution)/shard_map/pallas_call | solution.py:318
  102.1 5.3 %shard_map.177 = (f32[128,2048]{1,0:T(8,128)S(1)}, bf16[128,2048]{1,0:T(8,128)(2,1)S(1)}, bf16[128,2048]{1,0:T(8,128)(2,1)S(1)}, bf16[128,2048]{1,0:T(8,128)(2,1...) custom-call(bf16[512,256]{1,0:T(8,128)(2,1)S(1)} %get-tuple-element., ...), custom_call_target="tpu_custom_call" | custom-call | flops 2147483648 | bytes 9437184 | tf_op jit(solution)/shard_map/pallas_call | solution.py:355
  112.1 5.3 %collective-permute-done.15 = bf16[128,2048]{1,0:T(8,128)(2,1)S(1)} collective-permute-done((bf16[128,2048]{1,0:T(8,128)(2,1)S(1)}, bf16[128,2048]{1,0:T(8,128)(2,1)S(1)}, u32[]{:S(2)}, u32[]{:S(2)}) %collective-permute-start.15) | collective-permute-done | bytes 524320 | tf_op jit(solution)/shard_map/ppermute | solution.py:132
  118.7 4.3 %collective-permute-done.16 = bf16[128,2048]{1,0:T(8,128)(2,1)S(1)} collective-permute-done((bf16[128,2048]{1,0:T(8,128)(2,1)S(1)}, bf16[128,2048]{1,0:T(8,128)(2,1)S(1)}, u32[]{:S(2)}, u32[]{:S(2)}) %collective-permute-start.16) | collective-permute-done | bytes 524320 | tf_op jit(solution)/shard_map/ppermute | solution.py:132
  124.1 5.3 %all-to-all-start.2 = ((bf16[16,8,2048]{2,1,0:T(8,128)(2,1)}), bf16[16,8,2048]{2,1,0:T(8,128)(2,1)}, u32[]{:S(2)}, u32[]{:S(2)}) async-start(bf16[16,8,2048]{2,1,0:T(8,128)(2,1)} %fusion.22), calls=%async_computation.2 | async-start | bytes 1048576 | tf_op jit(solution)/shard_map/all_to_all | solution.py:155
  129.4 4.9 %collective-permute-done.19 = bf16[128,2048]{1,0:T(8,128)(2,1)} collective-permute-done((bf16[128,2048]{1,0:T(8,128)(2,1)S(1)}, bf16[128,2048]{1,0:T(8,128)(2,1)}, u32[]{:S(2)}, u32[]{:S(2)}) %collective-permute-start.19) | collective-permute-done | bytes 524320 | tf_op jit(solution)/shard_map/ppermute | solution.py:132
  134.3 2.5 %fusion.23 = bf16[16,8,2048]{2,1,0:T(8,128)(2,1)} fusion(bf16[128,2048]{1,0:T(8,128)(2,1)} %collective-permute-done.20, bf16[128,2048]{1,0:T(8,128)(2,1)} %collective-permute-done.19, f32[128,2048]{1,0:T(8,128)S(1)} %get-tuple-element.49, bf16[128,2048]{1,0:T(8,128)(2,1)} %collective-permute-done.18), kind=kLoop, calls=%fused_computation.27 | loop fusion | flops 1835008 | bytes 3145728 | tf_op jit(solution)/shard_map/reshape | solution.py:505
  136.8 3.1 %all-to-all-done.2 = bf16[16,8,2048]{2,1,0:T(8,128)(2,1)} async-done(((bf16[16,8,2048]{2,1,0:T(8,128)(2,1)}), bf16[16,8,2048]{2,1,0:T(8,128)(2,1)}, u32[]{:S(2)}, u32[]{:S(2)}) %all-to-all-start.2) | async-done | bytes 524320 | tf_op jit(solution)/shard_map/all_to_all | solution.py:155
  139.9 4.0 %all-to-all-start.3 = ((bf16[16,8,2048]{2,1,0:T(8,128)(2,1)}), bf16[16,8,2048]{2,1,0:T(8,128)(2,1)S(1)}, u32[]{:S(2)}, u32[]{:S(2)}) async-start(bf16[16,8,2048]{2,1,0:T(8,128)(2,1)} %fusion.23), calls=%async_computation.3 | async-start | bytes 1048576 | tf_op jit(solution)/shard_map/all_to_all | solution.py:155
  145.0 8.4 %all-to-all-done.3 = bf16[16,8,2048]{2,1,0:T(8,128)(2,1)S(1)} async-done(((bf16[16,8,2048]{2,1,0:T(8,128)(2,1)}), bf16[16,8,2048]{2,1,0:T(8,128)(2,1)S(1)}, u32[]{:S(2)}, u32[]{:S(2)}) %all-to-all-start.3) | async-done | bytes 524320 | tf_op jit(solution)/shard_map/all_to_all | solution.py:155
  153.5 2.6 %collective-permute-start.21 = (bf16[4,4096]{1,0:T(4,128)(2,1)S(1)}, bf16[4,4096]{1,0:T(4,128)(2,1)S(1)}, u32[]{:S(2)}, u32[]{:S(2)}) collective-permute-start(bf16[4,4096]{1,0:T(4,128)(2,1)S(1)} %constant_dynamic-slice_fusion), channel_id=1, source_target_pairs={{0,64},{64,0},{1,65},{65,1},{2,66},{66,2},{3,67},{67,3},{4,68},{68... | collective-permute-start | bytes 98312 | tf_op jit(solution)/shard_map/ppermute | solution.py:136
  (129 shorter events, 39.0 us)
Async XLA Ops:
  1.2 8.1 %collective-permute-start = (bf16[32,4096]{1,0:T(8,128)(2,1)S(1)}, bf16[32,4096]{1,0:T(8,128)(2,1)S(1)}, u32[]{:S(2)}, u32[]{:S(2)}) collective-permute-start(bf16[32,4096]{1,0:T(8,128)(2,1)S(1)} %get-tuple-element.60), channel_id=1, source_target_pairs={{0,64},{64,0},{1,65},{65,1},{2,66},{66,2},{3,67},{67,3},{4,68},{68... | collective-permute-start | bytes 786440 | tf_op jit(solution)/shard_map/ppermute | solution.py:136
  9.4 24.4 %collective-permute-start.1 = (bf16[64,4096]{1,0:T(8,128)(2,1)S(1)}, bf16[64,4096]{1,0:T(8,128)(2,1)S(1)}, u32[]{:S(2)}, u32[]{:S(2)}) collective-permute-start(bf16[64,4096]{1,0:T(8,128)(2,1)S(1)} %get-tuple-element.58), channel_id=1, source_target_pairs={{0,32},{1,33},{2,34},{3,35},{4,36},{5,37},{6,38},{7,39},{8,40},{9,... | collective-permute-start | bytes 1572872 | tf_op jit(solution)/shard_map/ppermute | solution.py:132
  13.6 22.9 %all-to-all-start = ((bf16[16,8,4096]{2,1,0:T(8,128)(2,1)}), bf16[16,8,4096]{2,1,0:T(8,128)(2,1)S(1)}, u32[]{:S(2)}, u32[]{:S(2)}) async-start(bf16[16,8,4096]{2,1,0:T(8,128)(2,1)} %broadcast_in_dim.46), calls=%async_computation | async-start | bytes 2097152 | tf_op jit(solution)/shard_map/all_to_all | solution.py:155
  37.6 15.2 %collective-permute-start.2 = (bf16[128,4096]{1,0:T(8,128)(2,1)S(1)}, bf16[128,4096]{1,0:T(8,128)(2,1)S(1)}, u32[]{:S(2)}, u32[]{:S(2)}) collective-permute-start(bf16[128,4096]{1,0:T(8,128)(2,1)S(1)} %fusion.18.x0.refs_0_), channel_id=1, source_target_pairs={{0,16},{1,17},{2,18},{3,19},{4,20},{5,21},{6,22},{7,23},{8,24},{9,... | collective-permute-start | bytes 3145736 | tf_op jit(solution)/shard_map/ppermute | solution.py:132
  38.3 16.8 %collective-permute-start.3 = (bf16[128,4096]{1,0:T(8,128)(2,1)S(1)}, bf16[128,4096]{1,0:T(8,128)(2,1)}, u32[]{:S(2)}, u32[]{:S(2)}) collective-permute-start(bf16[128,4096]{1,0:T(8,128)(2,1)S(1)} %fusion.18.x0.refs_0_), channel_id=1, source_target_pairs={{0,48},{1,49},{2,50},{3,51},{4,52},{5,53},{6,54},{7,55},{8,56},{9,... | collective-permute-start | bytes 3145736 | tf_op jit(solution)/shard_map/ppermute | solution.py:132
  40.4 60.2 %collective-permute-start.14 = (bf16[256,4096]{1,0:T(8,128)(2,1)}, bf16[256,4096]{1,0:T(8,128)(2,1)}, u32[]{:S(2)}, u32[]{:S(2)}) collective-permute-start(bf16[256,4096]{1,0:T(8,128)(2,1)} %copy-done.13), channel_id=1, source_target_pairs={{0,64},{64,0},{1,65},{65,1},{2,66},{66,2},{3,67},{67,3},{4,68},{68... | collective-permute-start | bytes 6291464 | tf_op jit(solution)/shard_map/ppermute | solution.py:136
  43.1 24.2 %collective-permute-start.4 = (bf16[128,4096]{1,0:T(8,128)(2,1)S(1)}, bf16[128,4096]{1,0:T(8,128)(2,1)}, u32[]{:S(2)}, u32[]{:S(2)}) collective-permute-start(bf16[128,4096]{1,0:T(8,128)(2,1)S(1)} %fusion.18.x0.refs_0_), channel_id=1, source_target_pairs={{0,64},{64,0},{1,65},{65,1},{2,66},{66,2},{3,67},{67,3},{4,68},{68... | collective-permute-start | bytes 3145736 | tf_op jit(solution)/shard_map/ppermute | solution.py:136
  52.9 14.5 %collective-permute-start.5 = (bf16[128,4096]{1,0:T(8,128)(2,1)S(1)}, bf16[128,4096]{1,0:T(8,128)(2,1)}, u32[]{:S(2)}, u32[]{:S(2)}) collective-permute-start(bf16[128,4096]{1,0:T(8,128)(2,1)S(1)} %collective-permute-done.2.x1.refs_1_), channel_id=1, source_target_pairs={{0,64},{64,0},{1,65},{65,1},{2,66},{66,2},{3,67},{67,3},{4,68},{68... | collective-permute-start | bytes 3145736 | tf_op jit(solution)/shard_map/ppermute | solution.py:136
  55.1 12.2 %collective-permute-start.6 = (bf16[128,4096]{1,0:T(8,128)(2,1)}, bf16[128,4096]{1,0:T(8,128)(2,1)}, u32[]{:S(2)}, u32[]{:S(2)}) collective-permute-start(bf16[128,4096]{1,0:T(8,128)(2,1)} %collective-permute-done.3.x3.refs_2_), channel_id=1, source_target_pairs={{0,64},{64,0},{1,65},{65,1},{2,66},{66,2},{3,67},{67,3},{4,68},{68... | collective-permute-start | bytes 3145736 | tf_op jit(solution)/shard_map/ppermute | solution.py:136
  59.5 18.0 %all-to-all-start.1 = ((f32[16,16,384]{2,1,0:T(8,128)}), f32[16,16,384]{2,1,0:T(8,128)}, u32[]{:S(2)}, u32[]{:S(2)}) async-start(f32[16,16,384]{2,1,0:T(8,128)} %shard_map.173), calls=%async_computation.1 | async-start | bytes 786432 | tf_op jit(solution)/shard_map/all_to_all | solution.py:155
  65.4 17.3 %collective-permute-start.7 = (bf16[128,4096]{1,0:T(8,128)(2,1)S(1)}, bf16[128,4096]{1,0:T(8,128)(2,1)S(1)}, u32[]{:S(2)}, u32[]{:S(2)}) collective-permute-start(bf16[128,4096]{1,0:T(8,128)(2,1)S(1)} %collective-permute-done.2.x1.refs_1_), channel_id=1, source_target_pairs={{0,16},{1,17},{2,18},{3,19},{4,20},{5,21},{6,22},{7,23},{8,24},{9,... | collective-permute-start | bytes 3145736 | tf_op jit(solution)/shard_map/ppermute | solution.py:132
  82.8 8.8 %collective-permute-start.8 = (bf16[128,4096]{1,0:T(8,128)(2,1)S(1)}, bf16[128,4096]{1,0:T(8,128)(2,1)S(1)}, u32[]{:S(2)}, u32[]{:S(2)}) collective-permute-start(bf16[128,4096]{1,0:T(8,128)(2,1)S(1)} %pad_add_fusion), channel_id=1, source_target_pairs={{0,64},{64,0},{1,65},{65,1},{2,66},{66,2},{3,67},{67,3},{4,68},{68... | collective-permute-start | bytes 3145736 | tf_op jit(solution)/shard_map/ppermute | solution.py:136
  83.3 3.7 %collective-permute-start.10 = (f32[16,384]{1,0:T(8,128)S(1)}, f32[16,384]{1,0:T(8,128)S(1)}, u32[]{:S(2)}, u32[]{:S(2)}) collective-permute-start(f32[16,384]{1,0:T(8,128)S(1)} %add_reduce_fusion), channel_id=1, source_target_pairs={{0,48},{1,49},{2,50},{3,51},{4,52},{5,53},{6,54},{7,55},{8,56},{9,... | collective-permute-start | bytes 73736 | tf_op jit(solution)/shard_map/ppermute | solution.py:132
  85.8 4.2 %collective-permute-start.11 = (f32[16,384]{1,0:T(8,128)S(1)}, f32[16,384]{1,0:T(8,128)S(1)}, u32[]{:S(2)}, u32[]{:S(2)}) collective-permute-start(f32[16,384]{1,0:T(8,128)S(1)} %add_reduce_fusion), channel_id=1, source_target_pairs={{0,32},{1,33},{2,34},{3,35},{4,36},{5,37},{6,38},{7,39},{8,40},{9,... | collective-permute-start | bytes 73736 | tf_op jit(solution)/shard_map/ppermute | solution.py:132
  86.4 4.2 %collective-permute-start.9 = (f32[16,384]{1,0:T(8,128)S(1)}, f32[16,384]{1,0:T(8,128)S(1)}, u32[]{:S(2)}, u32[]{:S(2)}) collective-permute-start(f32[16,384]{1,0:T(8,128)S(1)} %add_reduce_fusion), channel_id=1, source_target_pairs={{0,16},{1,17},{2,18},{3,19},{4,20},{5,21},{6,22},{7,23},{8,24},{9,... | collective-permute-start | bytes 73736 | tf_op jit(solution)/shard_map/ppermute | solution.py:132
  90.6 6.3 %collective-permute-start.12 = (f32[16,512]{1,0:T(8,128)S(1)}, f32[16,512]{1,0:T(8,128)S(1)}, u32[]{:S(2)}, u32[]{:S(2)}) collective-permute-start(f32[16,512]{1,0:T(8,128)S(1)} %pad_maximum_fusion.2.low_ref), channel_id=1, source_target_pairs={{0,64},{64,0},{1,65},{65,1},{2,66},{66,2},{3,67},{67,3},{4,68},{68... | collective-permute-start | bytes 98312 | tf_op jit(solution)/shard_map/ppermute | solution.py:136
  107.4 10.0 %collective-permute-start.15 = (bf16[128,2048]{1,0:T(8,128)(2,1)S(1)}, bf16[128,2048]{1,0:T(8,128)(2,1)S(1)}, u32[]{:S(2)}, u32[]{:S(2)}) collective-permute-start(bf16[128,2048]{1,0:T(8,128)(2,1)S(1)} %get-tuple-element.46), channel_id=1, source_target_pairs={{0,32},{1,33},{2,34},{3,35},{4,36},{5,37},{6,38},{7,39},{8,40},{9,... | collective-permute-start | bytes 1572872 | tf_op jit(solution)/shard_map/ppermute | solution.py:132
  108.9 14.1 %collective-permute-start.16 = (bf16[128,2048]{1,0:T(8,128)(2,1)S(1)}, bf16[128,2048]{1,0:T(8,128)(2,1)S(1)}, u32[]{:S(2)}, u32[]{:S(2)}) collective-permute-start(bf16[128,2048]{1,0:T(8,128)(2,1)S(1)} %get-tuple-element.47), channel_id=1, source_target_pairs={{0,16},{1,17},{2,18},{3,19},{4,20},{5,21},{6,22},{7,23},{8,24},{9,... | collective-permute-start | bytes 1572872 | tf_op jit(solution)/shard_map/ppermute | solution.py:132
  109.4 13.6 %collective-permute-start.17 = (bf16[128,2048]{1,0:T(8,128)(2,1)S(1)}, bf16[128,2048]{1,0:T(8,128)(2,1)S(1)}, u32[]{:S(2)}, u32[]{:S(2)}) collective-permute-start(bf16[128,2048]{1,0:T(8,128)(2,1)S(1)} %get-tuple-element.48), channel_id=1, source_target_pairs={{0,48},{1,49},{2,50},{3,51},{4,52},{5,53},{6,54},{7,55},{8,56},{9,... | collective-permute-start | bytes 1572872 | tf_op jit(solution)/shard_map/ppermute | solution.py:132
  111.5 17.8 %collective-permute-start.18 = (bf16[128,2048]{1,0:T(8,128)(2,1)S(1)}, bf16[128,2048]{1,0:T(8,128)(2,1)}, u32[]{:S(2)}, u32[]{:S(2)}) collective-permute-start(bf16[128,2048]{1,0:T(8,128)(2,1)S(1)} %get-tuple-element.50), channel_id=1, source_target_pairs={{0,32},{1,33},{2,34},{3,35},{4,36},{5,37},{6,38},{7,39},{8,40},{9,... | collective-permute-start | bytes 1572872 | tf_op jit(solution)/shard_map/ppermute | solution.py:132
  111.9 22.4 %collective-permute-start.19 = (bf16[128,2048]{1,0:T(8,128)(2,1)S(1)}, bf16[128,2048]{1,0:T(8,128)(2,1)}, u32[]{:S(2)}, u32[]{:S(2)}) collective-permute-start(bf16[128,2048]{1,0:T(8,128)(2,1)S(1)} %get-tuple-element.51), channel_id=1, source_target_pairs={{0,16},{1,17},{2,18},{3,19},{4,20},{5,21},{6,22},{7,23},{8,24},{9,... | collective-permute-start | bytes 1572872 | tf_op jit(solution)/shard_map/ppermute | solution.py:132
  117.4 16.9 %collective-permute-start.20 = (bf16[128,2048]{1,0:T(8,128)(2,1)S(1)}, bf16[128,2048]{1,0:T(8,128)(2,1)}, u32[]{:S(2)}, u32[]{:S(2)}) collective-permute-start(bf16[128,2048]{1,0:T(8,128)(2,1)S(1)} %get-tuple-element.52), channel_id=1, source_target_pairs={{0,48},{1,49},{2,50},{3,51},{4,52},{5,53},{6,54},{7,55},{8,56},{9,... | collective-permute-start | bytes 1572872 | tf_op jit(solution)/shard_map/ppermute | solution.py:132
  124.1 15.8 %all-to-all-start.2 = ((bf16[16,8,2048]{2,1,0:T(8,128)(2,1)}), bf16[16,8,2048]{2,1,0:T(8,128)(2,1)}, u32[]{:S(2)}, u32[]{:S(2)}) async-start(bf16[16,8,2048]{2,1,0:T(8,128)(2,1)} %fusion.22), calls=%async_computation.2 | async-start | bytes 1048576 | tf_op jit(solution)/shard_map/all_to_all | solution.py:155
  139.9 13.5 %all-to-all-start.3 = ((bf16[16,8,2048]{2,1,0:T(8,128)(2,1)}), bf16[16,8,2048]{2,1,0:T(8,128)(2,1)S(1)}, u32[]{:S(2)}, u32[]{:S(2)}) async-start(bf16[16,8,2048]{2,1,0:T(8,128)(2,1)} %fusion.23), calls=%async_computation.3 | async-start | bytes 1048576 | tf_op jit(solution)/shard_map/all_to_all | solution.py:155
  (22 other events, 207.6 us)
